TPU v7x, 32 devices: a whole 2x2x4 slice. The times are simulated.
32 devices in a mesh: groups: 2 (over y), tensor: 4 (over z), dp: 4 (over x, core).
Axes of the slice: x: 2, y: 2, z: 4, core: 2. Of those that a mesh axis runs over, the one named last changes fastest.
Arguments:
- out_grad: bfloat16 [4, 1280, 4096], P('dp', ('groups', 'tensor')), parts along dimension 1, may hold values from -6 to 6
- gate_pre: bfloat16 [4, 1280, 14336], P('dp', 'groups', 'tensor'), parts along dimension 1, may hold values from -8 to 8
- up_pre: bfloat16 [4, 1280, 14336], P('dp', 'groups', 'tensor'), parts along dimension 1, may hold values from -6 to 6
- down_weight: bfloat16 [14336, 4096], P('tensor'), may hold values from -0.046875 to 0.046875
Outputs:
- gate_grad: bfloat16 [4, 1280, 14336], P('dp', 'groups', 'tensor'), parts along dimension 1
- up_grad: bfloat16 [4, 1280, 14336], P('dp', 'groups', 'tensor'), parts along dimension 1
- down_grad: bfloat16 [28672, 4096], P(('groups', 'tensor'), 'dp'), parts along dimension 0
There are 2 independent parts, one for each index of `groups`. A program takes and returns all parts, laid end to end along the dimension named above; an argument that names none is the same for every part. Nothing has to cross between parts.
All inputs are finite; a program needn't handle non-finite values.
Results may differ from a plain program's by a relative error of at most 0.014.
Values may be sent and summed in bfloat16 or wider, within the bound.
No kernel may reach another device: no remote copies, remote signals or barrier semaphores. Data moves between devices by JAX's collectives and lax.ppermute only.
A program may use at most 128 MiB of HBM per device.

v0:
```python
import math

import jax
import jax.numpy as jnp
from jax import lax
from jax.sharding import PartitionSpec as P


def times_down(block, down_weight):
    return lax.dot_general(
        block, down_weight, (((1,), (1,)), ((), ())), preferred_element_type=jnp.float32
    )


def on_device(out_grad, gate_pre, up_pre, down_weight):
    gate = gate_pre[0].astype(jnp.float32)
    up = up_pre[0].astype(jnp.float32)
    sig = jax.nn.sigmoid(gate)
    act = gate * sig
    hidden = (act * up).astype(jnp.bfloat16)
    group_rows = hidden.shape[0]
    scale = 1.0 / math.sqrt(group_rows * lax.axis_size("dp"))
    block = lax.all_gather(out_grad, "tensor", axis=1, tiled=True)[0]
    weight_acc = jnp.einsum("tf,td->fd", hidden, block, preferred_element_type=jnp.float32)
    hidden_grad = times_down(block, down_weight)
    weight_acc, hidden_grad = (weight_acc, hidden_grad)
    down_grad = lax.psum_scatter(
        (weight_acc * scale).astype(jnp.bfloat16), "dp", scatter_dimension=1, tiled=True
    )
    gate_grad = (hidden_grad * up * sig * (1.0 + gate * (1.0 - sig))).astype(jnp.bfloat16)
    up_grad = (hidden_grad * act).astype(jnp.bfloat16)
    return (gate_grad[None], up_grad[None], down_grad)


def solution(mesh):
    return jax.shard_map(
        on_device,
        mesh=mesh,
        in_specs=(
            P("dp", ("groups", "tensor"), None),
            P("dp", "groups", "tensor"),
            P("dp", "groups", "tensor"),
            P("tensor", None),
        ),
        out_specs=(
            P("dp", "groups", "tensor"),
            P("dp", "groups", "tensor"),
            P(("groups", "tensor"), "dp"),
        ),
        check_vma=False,
    )
```

profile of v0, /device:TPU:0, one launch (start us, length us, event | category | flops | bytes accessed | tf_op | source)
XLA Modules:
  0.0 359.5 jit_solution(4585248660754477539)
XLA Ops:
  7.2 0.0 all-gather.2.cloned.1.call-start
  7.2 0.7 all-gather.2.cloned.1.call-update
  7.9 0.0 reduce-scatter.2.cloned.1.call-start
  7.9 102.4 %all-gather.2.cloned.1.call-done = bf16[1,640,4096]{2,1,0:T(8,128)(2,1)} async-done(((bf16[1,160,4096]{2,1,0:T(8,128)(2,1)}), bf16[1,640,4096]{2,1,0:T(8,128)(2,1)}) %all-gather.2.cloned.1.call-update) | async-done | bytes 5242896 | tf_op jit(solution)/shard_map/all_gather | solution.py:23
  110.4 35.9 %multiply_convert_fusion = bf16[3584,4096]{1,0:T(8,128)(2,1)} fusion(bf16[1,640,4096]{2,1,0:T(8,128)(2,1)} %all-gather.2.cloned.1.call-done, bf16[1,640,3584]{2,1,0:T(8,128)(2,1)} %param.6, bf16[1,640,3584]{2,1,0:T(8,128)(2,1)} %param.5), kind=kOutput, calls=%fused_computation | convolution fusion | flops 18838192128 | bytes 43778048 | tf_op jit(solution)/shard_map/tf,td->fd/dot_general | solution.py:24
  146.3 0.0 reduce-scatter.2.cloned.1.call-update
  146.3 34.0 %fusion.22 = (bf16[1,640,3584]{2,1,0:T(8,128)(2,1)}, bf16[1,640,3584]{2,1,0:T(8,128)(2,1)}) fusion(bf16[1,640,3584]{2,1,0:T(8,128)(2,1)} %param.5, bf16[1,640,3584]{2,1,0:T(8,128)(2,1)} %param.6, bf16[3584,4096]{1,0:T(8,128)(2,1)} %param.7, bf16[1,640,4096]{2,1,0:T(8,128)(2,1)} %all-gather.2.cloned.1.call-done), kind=kOutput, calls=%fused_computation.27 | convolution fusion | flops 18824888320 | bytes 52953088 | tf_op jit(solution)/shard_map/dot_general | solution.py:10
  180.3 172.4 %reduce-scatter.2.cloned.1.call-done = bf16[3584,1024]{1,0:T(8,128)(2,1)} async-done(((bf16[3584,4096]{1,0:T(8,128)(2,1)}), bf16[3584,1024]{1,0:T(8,128)(2,1)}) %reduce-scatter.2.cloned.1.call-update) | async-done | bytes 7340048 | tf_op jit(solution)/shard_map/reduce_scatter | solution.py:27
Async XLA Ops:
  7.2 103.2 %all-gather.2.cloned.1.call-start = ((), (), s32[]{:S(2)}) async-start(), calls=%async_computation.1 | async-start | bytes 6553600 | tf_op jit(solution)/shard_map/all_gather | solution.py:23
  7.9 344.8 %reduce-scatter.2.cloned.1.call-start = ((), (), s32[]{:S(2)}) async-start(), calls=%async_computation.2 | async-start | bytes 36700160 | tf_op jit(solution)/shard_map/reduce_scatter | solution.py:27
Sparse Core Ops, SparseCore 0:
  9.6 100.7 all-gather.1
  146.4 206.2 reduce-scatter.1
where the time goes:
time: 360 us
  waiting for transfers between devices  275 us (76%)
  matrix products  69.9 us (19%)
  between operations  14 us (4%)
    reduce_scatter x1, waiting for transfers between devices, on_device(): lax.psum_scatter((weight_acc * scale).astype(jnp.bfloat16), 'dp', scatter...  172 us
    all_gather x1, waiting for transfers between devices, on_device(): block = lax.all_gather(out_grad, 'tensor', axis=1, tiled=True)[0]  102 us
    dot_general x1, matrix products, on_device(): jnp.einsum('tf,td->fd', hidden, block, preferred_element_type=jnp.float32)  35.9 us
    dot_general x1, matrix products, times_down(): lax.dot_general(block, down_weight, (((1,), (1,)), ((), ())), preferred_e...  34 us
  transfers between devices with their start and end apart: 2, of which 2 were waited for; matrix products, arithmetic and copies ran while one was open for 9% of the time, Pallas kernels for 0%

commit v1 on v0

v1 whole, which is shorter than its diff:
```python
import functools
import math

import jax
import jax.numpy as jnp
from jax import lax
from jax.experimental import pallas as pl
from jax.experimental.pallas import tpu as pltpu
from jax.sharding import PartitionSpec as P

VMEM_LIMIT = 16 * 1024 * 1024
F32, BF16 = jnp.float32, jnp.bfloat16
ANY_SPEC = pl.BlockSpec(memory_space=pl.ANY)
VMEM_SPEC = pl.BlockSpec(memory_space=pltpu.VMEM)


def pick_tile(extent, cap):
    return max(t for t in range(128, cap + 1, 128) if extent % t == 0)


def together(*values):
    return lax.optimization_barrier(values)


def sigmoid(x):
    return 0.5 + 0.5 * jnp.tanh(0.5 * x)


def contract_last(a, b):
    return lax.dot_general(a, b, (((1,), (1,)), ((), ())), preferred_element_type=F32)


def contract_first(a, b):
    return lax.dot_general(a, b, (((0,), (0,)), ((), ())), preferred_element_type=F32)


def in_vmem(value):
    return pltpu.with_memory_space_constraint(value, pltpu.VMEM)


def in_hbm(values):
    return [pltpu.with_memory_space_constraint(v, pltpu.HBM) for v in values]


def place_shards(parts, half, into, sem, start):
    act = (lambda c: c.start()) if start else (lambda c: c.wait())
    z = lax.axis_index("tensor")
    rows = parts[0].shape[0]

    def place(ref, shard, slot):
        at = shard if half == "all" else shard % 2
        at = pl.multiple_of(at * rows, rows)
        act(pltpu.make_async_copy(ref, into.at[pl.ds(at, rows)], sem.at[slot]))

    if half != "late":
        place(parts[0], z, 0)
        place(parts[1], z + 1 - 2 * (z % 2), 1)
    if half != "early":
        b0, b1, c0, c1 = parts[-4:]
        first, second = jnp.where(z < 2, 2, 1), jnp.where(z < 2, 3, 0)
        middle = jnp.logical_or(z == 1, z == 2)

        @pl.when(middle)
        def _():
            place(b0, first, 2)
            place(b1, second, 3)

        @pl.when(jnp.logical_not(middle))
        def _():
            place(c0, first, 2)
            place(c1, second, 3)


def move_kernel(n_parts, *refs):
    parts, (into, sem) = refs[:n_parts], refs[-2:]
    first = refs[n_parts : -2]
    rows = 4 * parts[0].shape[0]
    if first:
        copy = pltpu.make_async_copy(first[0], into.at[pl.ds(0, rows)], sem.at[4])
        copy.start()
        into = into.at[pl.ds(rows, rows)]
    for start in (True, False):
        place_shards(parts, "all", into, sem, start)
    if first:
        copy.wait()


def in_token_order(parts, first=()):
    rows, cols = parts[0].shape
    return pl.pallas_call(
        functools.partial(move_kernel, len(parts)),
        in_specs=[ANY_SPEC] * len(parts) + [VMEM_SPEC] * len(first),
        out_specs=VMEM_SPEC,
        out_shape=pltpu.VMEM((rows * 4 * (1 + len(first)), cols), BF16),
        scratch_shapes=[pltpu.SemaphoreType.DMA((5,))],
        compiler_params=pltpu.CompilerParams(vmem_limit_bytes=VMEM_LIMIT),
        name="in_token_order",
    )(*parts, *[in_vmem(f) for f in first])


def load_weight_kernel(weight, *refs):
    outs, mark, sem = refs[:-2], refs[-2], refs[-1]
    chip = lax.axis_index("dp") // 2
    copies = []
    for s, out in enumerate(outs):
        width = out.shape[1]
        at = pl.multiple_of(lax.rem(chip + s, len(outs)) * width, width)
        copies.append(pltpu.make_async_copy(weight.at[:, pl.ds(at, width)], out, sem.at[s]))
    for copy in copies:
        copy.start()
    mark[...] = jnp.zeros(mark.shape, mark.dtype)
    for copy in copies:
        copy.wait()


def load_weight(weight, blocks):
    ff, d = weight.shape
    return pl.pallas_call(
        load_weight_kernel,
        in_specs=[ANY_SPEC],
        out_specs=[VMEM_SPEC] * (blocks + 1),
        out_shape=[pltpu.VMEM((ff, d // blocks), BF16)] * blocks + [jax.ShapeDtypeStruct((8, 128), F32)],
        scratch_shapes=[pltpu.SemaphoreType.DMA((blocks,))],
        cost_estimate=pl.CostEstimate(flops=0, bytes_accessed=4 * ff * d, transcendentals=0),
        compiler_params=pltpu.CompilerParams(vmem_limit_bytes=VMEM_LIMIT),
        name="load_weight",
    )(*in_hbm([weight]))


def hidden_kernel(gate_ref, up_ref, hidden_ref):
    gate, up = gate_ref[...].astype(F32), up_ref[...].astype(F32)
    hidden_ref[...] = (gate * sigmoid(gate) * up).astype(BF16)


def factors_kernel(start, gate_ref, up_ref, hidden_ref, gate_by_ref, up_by_ref):
    gate, up = gate_ref[...].astype(F32), up_ref[...].astype(F32)
    sig = sigmoid(gate)
    act = gate * sig
    gate_by_ref[...] = (up * sig * (1.0 + gate * (1.0 - sig))).astype(BF16)
    up_by_ref[...] = act.astype(BF16)
    hidden_ref[...] = (act[:, start:] * up[:, start:]).astype(BF16)


def factors(kernel, gate, up, columns, widths):
    tok = gate.shape[0]
    rows = next(r for r in (64, 32, 16) if tok % r == 0)
    spec = lambda w: pl.BlockSpec((rows, w), lambda i: (i, 0))
    return pl.pallas_call(
        kernel,
        grid=(tok // rows,),
        in_specs=[spec(columns)] * 2,
        out_specs=[spec(w) for w in widths],
        out_shape=[pltpu.HBM((tok, w), BF16) for w in widths],
        cost_estimate=pl.CostEstimate(
            flops=20 * tok * columns, bytes_accessed=2 * tok * (2 * columns + sum(widths)), transcendentals=tok * columns
        ),
        compiler_params=pltpu.CompilerParams(vmem_limit_bytes=VMEM_LIMIT),
        name="factors",
    )(*in_hbm([gate, up]))


def hidden_grad_kernel(half, counts, tile, has_partial, finish, *refs):
    refs = list(refs)
    streams = [[refs.pop(0) for _ in range(count)] for count in counts]
    weights = [refs.pop(0) for _ in counts]
    partial = refs.pop(0) if has_partial else None
    if half == "all":
        lhs = [stream[0] for stream in streams]
    else:
        sem = refs.pop()
        lhs = refs[-len(counts) :]
        refs = refs[: -len(counts)]

        @pl.when(pl.program_id(0) == 0)
        def _():
            for start in (True, False):
                for s, parts in enumerate(streams):
                    place_shards(parts, half, lhs[s], sem.at[s], start)

    at = pl.multiple_of(pl.program_id(0) * tile, tile)
    total = partial[...] if has_partial else None
    for left, weight in zip(lhs, weights):
        term = contract_last(left[...], weight[pl.ds(at, tile), :])
        total = term if total is None else total + term
    if not finish:
        refs[-1][...] = total
        return
    gate_out, up_out = refs[-2:]
    gate_out[...] = (total * refs[0][...].astype(F32)).astype(BF16)
    up_out[...] = (total * refs[1][...].astype(F32)).astype(BF16)


def hidden_grad(half, streams, weights, tok, partial=None, by=None, outs=None):
    ff = weights[0].shape[0]
    rows = tok if half == "all" else tok // 2
    tile = pick_tile(ff, 896)

    def place(i):
        pair = lax.axis_index("tensor") // 2
        return ({"all": 0, "early": pair, "late": 1 - pair}[half], i)

    block = pl.BlockSpec((rows, tile), place)
    part_block = pl.BlockSpec((rows, tile), lambda i: (0, i))
    if half == "all":
        in_specs, args, scratch = [VMEM_SPEC] * len(streams), [in_vmem(s[0]) for s in streams], []
    else:
        args = [part for s in streams for part in s]
        in_specs = [ANY_SPEC] * len(args)
        scratch = [pltpu.VMEM((rows, w.shape[1]), BF16) for w in weights] + [
            pltpu.SemaphoreType.DMA((len(weights), 4))
        ]
    in_specs += [VMEM_SPEC] * len(weights)
    args += [in_vmem(w) for w in weights]
    aliases = {}
    if partial is not None:
        in_specs.append(part_block)
        args += in_hbm([partial])
    if by is not None:
        in_specs += [block] * 2
        args += in_hbm(by)
        out_shape, out_specs = [pltpu.HBM((tok, ff), BF16)] * 2, [block] * 2
        if outs is not None:
            aliases = {len(args): 0, len(args) + 1: 1}
            in_specs += [ANY_SPEC] * 2
            args += in_hbm(outs)
    else:
        out_shape, out_specs = pltpu.HBM((rows, ff), F32), part_block
    return pl.pallas_call(
        functools.partial(
            hidden_grad_kernel, half, tuple(len(s) for s in streams), tile, partial is not None, by is not None
        ),
        grid=(ff // tile,),
        in_specs=in_specs,
        out_specs=out_specs,
        scratch_shapes=scratch,
        out_shape=out_shape,
        input_output_aliases=aliases,
        cost_estimate=pl.CostEstimate(
            flops=2 * rows * ff * sum(w.shape[1] for w in weights), bytes_accessed=12 * rows * ff, transcendentals=0
        ),
        compiler_params=pltpu.CompilerParams(vmem_limit_bytes=VMEM_LIMIT),
        name="hidden_grad_" + half + ("" if by is not None else "_partial"),
    )(*args)


def weight_grad_kernel(n, *refs):
    hidden, block, send, keep = refs[:n], refs[n], refs[n + 1], refs[n + 2]
    half = send.shape[1]
    lhs = jnp.concatenate([h[...] for h in hidden], axis=0) if n > 1 else hidden[0][...]
    total = contract_first(lhs, block[...]).astype(BF16)
    core = lax.axis_index("dp") % 2

    @pl.when(core == 0)
    def _():
        keep[...] = total[:, :half]
        send[...] = total[:, half:]

    @pl.when(core == 1)
    def _():
        send[...] = total[:, :half]
        keep[...] = total[:, half:]


def weight_grad(block, hiddens):
    (tok, ff), half = hiddens[0].shape, block.shape[1] // 2
    tile = pick_tile(ff, 256)
    return pl.pallas_call(
        functools.partial(weight_grad_kernel, len(hiddens)),
        grid=(ff // tile,),
        in_specs=[pl.BlockSpec((tok, tile), lambda i: (0, i))] * len(hiddens) + [VMEM_SPEC],
        out_specs=[pl.BlockSpec((tile, half), lambda i: (i, 0))] * 2,
        out_shape=[pltpu.HBM((ff, half), BF16)] * 2,
        cost_estimate=pl.CostEstimate(
            flops=4 * block.shape[0] * ff * half, bytes_accessed=2 * ff * (block.shape[0] + 2 * half), transcendentals=0
        ),
        compiler_params=pltpu.CompilerParams(vmem_limit_bytes=VMEM_LIMIT),
        name="weight_grad",
    )(*in_hbm(hiddens), in_vmem(block))


def add_kernel(scale, a_ref, b_ref, *refs):
    refs[-1][...] = ((a_ref[...].astype(F32) + b_ref[...].astype(F32)) * scale).astype(BF16)


def add_rows(keep, got, scale, row, total_rows, out=None):
    rows, cols = keep.shape
    tile = pick_tile(math.gcd(rows, row), 512)
    first = row // tile
    spec = pl.BlockSpec((tile, cols), lambda i: (i, 0))
    in_specs, args, aliases = [spec, spec], [keep, got], {}
    if out is not None:
        aliases = {2: 0}
        in_specs.append(ANY_SPEC)
        args += in_hbm([out])
    return pl.pallas_call(
        functools.partial(add_kernel, scale),
        grid=(rows // tile,),
        in_specs=in_specs,
        out_specs=pl.BlockSpec((tile, cols), lambda i: (i + first, 0)),
        out_shape=pltpu.HBM((total_rows, cols), BF16),
        input_output_aliases=aliases,
        cost_estimate=pl.CostEstimate(flops=2 * rows * cols, bytes_accessed=6 * rows * cols, transcendentals=0),
        compiler_params=pltpu.CompilerParams(vmem_limit_bytes=VMEM_LIMIT),
        name="add_rows",
    )(*args)


def on_device(out_grad, gate_pre, up_pre, down_weight):
    grad, gate, up = out_grad[0], gate_pre[0], up_pre[0]
    tok, ff = gate.shape
    d = grad.shape[1]
    dp, nt = lax.axis_size("dp"), lax.axis_size("tensor")
    chips = dp // 2
    cols = d // chips
    chip, pair = lax.axis_index("dp") // 2, lax.axis_index("tensor") // 2
    scale = 1.0 / math.sqrt(tok * dp)

    def shift(value, s):
        return lax.ppermute(
            value, "dp", [(2 * c + k, 2 * ((c + s) % chips) + k) for c in range(chips) for k in range(2)]
        )

    def swap_cores(value):
        return lax.ppermute(value, "dp", [(k, k ^ 1) for k in range(dp)])

    def columns_of(which):
        return lax.dynamic_slice(grad, (0, which * cols), (grad.shape[0], cols))

    if nt == 4 and chips == 2 and ff % 896 == 0:
        cut = 5 * ff // 7
        both_ways = lambda *pairs: [q for a, b in pairs for q in ((a, b), (b, a))]
        swap_pair = lambda v: lax.ppermute(v, "tensor", both_ways((0, 1), (2, 3)))
        swap_middle = lambda v: lax.ppermute(v, "tensor", both_ways((1, 2)))
        to_ends = lambda v: lax.ppermute(v, "tensor", [(1, 0), (2, 3)])

        mine, rest = together(columns_of(chip), columns_of(1 - chip))
        far = shift(rest, 1)
        a1, b01 = swap_pair(mine), swap_middle(mine)
        (h0,) = factors(hidden_kernel, gate, up, cut, [cut])
        a1, b01, rest = together(a1, b01, rest)
        c01, b11 = to_ends(b01), swap_middle(a1)
        a2, b02 = swap_pair(rest), swap_middle(rest)

        far, h0, gate, up = together(far, h0, gate, up)
        h0_in = shift(h0, 1)
        a3, b03 = swap_pair(far), swap_middle(far)
        h1, *by = factors(functools.partial(factors_kernel, cut), gate, up, ff, [ff - cut, ff, ff])

        a2, h1, by, weight = together(a2, h1, by, down_weight)
        h1_in = shift(h1, 1)
        *weights, mark = load_weight(weight, chips)

        b11, mark = together(b11, mark)
        c11 = to_ends(b11)
        outs = hidden_grad("early", [[mine, a1], [rest, a2]], weights, tok, None, by)

        a3, b03, outs = together(a3, b03, outs)
        c03, b13 = to_ends(b03), swap_middle(a3)
        b13, c01, c11, a2, b02 = together(b13, c01, c11, a2, b02)
        c13, b12, c02 = to_ends(b13), swap_middle(a2), to_ends(b02)
        block = in_token_order([mine, a1, b01, b11, c01, c11])
        partial = hidden_grad("late", [[b01, b11, c01, c11]], weights[:1], tok)

        b12, partial = together(b12, partial)
        c12 = to_ends(b12)
        c03, c13, h0_in, partial = together(c03, c13, h0_in, partial)
        block = in_token_order([far, a3, b03, b13, c03, c13], [block])
        send0, keep0 = weight_grad(block, [h0, h0_in])
        send0, keep0, h1, h1_in = together(send0, keep0, h1, h1_in)
        got0 = swap_cores(send0)
        send1, keep1 = weight_grad(block, [h1, h1_in])
        send1, keep1, got0 = together(send1, keep1, got0)
        got1 = swap_cores(send1)
        down_grad = add_rows(keep0, got0, scale, 0, ff)
        c02, c12, down_grad, partial = together(c02, c12, down_grad, partial)
        outs = hidden_grad("late", [[b02, b12, c02, c12]], weights[1:], tok, partial, by, outs)
        got1, outs = together(got1, outs)
        down_grad = add_rows(keep1, got1, scale, cut, ff, down_grad)
    else:
        gather = lambda v: lax.all_gather(v, "tensor", axis=0, tiled=True)
        hidden, *by = factors(functools.partial(factors_kernel, 0), gate, up, ff, [ff, ff, ff])
        hiddens = [hidden] + [shift(hidden, s) for s in range(1, chips)]
        blocks = [gather(columns_of(chip))]
        blocks += [gather(shift(columns_of((chip + s) % chips), s)) for s in range(1, chips)]
        block = jnp.concatenate(blocks, axis=0)
        outs = hidden_grad("all", [[gather(grad)]], load_weight(down_weight, 1)[:1], tok, None, by)
        send, keep = weight_grad(block, hiddens)
        down_grad = add_rows(keep, swap_cores(send), scale, 0, ff)
    return (outs[0][None], outs[1][None], down_grad)


def solution(mesh):
    return jax.shard_map(
        on_device,
        mesh=mesh,
        in_specs=(
            P("dp", ("groups", "tensor"), None),
            P("dp", "groups", "tensor"),
            P("dp", "groups", "tensor"),
            P("tensor", None),
        ),
        out_specs=(
            P("dp", "groups", "tensor"),
            P("dp", "groups", "tensor"),
            P(("groups", "tensor"), "dp"),
        ),
        check_vma=False,
    )
```

time: 360 us -> 209 us (0.58)
  waiting for transfers between devices: 275 us -> 80.6 us
  Pallas kernels: 0 us -> 99.7 us
  matrix products: 69.9 us -> 0 us
  starting transfers between devices: 0.08 us -> 23.4 us
  between operations: 14 us -> 0.95 us
    reduce_scatter x1 -> x0, waiting for transfers between devices: 172 us -> none  [on_device(): lax.psum_scatter((weight_acc * scale).astype(jnp.bfloat16), 'dp', scatter...]
    all_gather x1 -> x0, waiting for transfers between devices: 102 us -> none  [on_device(): block = lax.all_gather(out_grad, 'tensor', axis=1, tiled=True)[0]]
    pallas_call x0 -> x12, Pallas kernels: none -> 99.7 us  [the longest x3 33.3 us: hidden_grad(): pl.pallas_call(functools.partial(hidden_grad_kernel, half, tuple((len(s)...]
    ppermute x0 -> x20, waiting for transfers between devices: none -> 80.6 us  [the longest x6 74.5 us: on_device(): to_ends = lambda v: lax.ppermute(v, 'tensor', [(1, 0), (2, 3)])]
    dot_general x2 -> x0, matrix products: 69.9 us -> none  [the longest x1 35.9 us: on_device(): jnp.einsum('tf,td->fd', hidden, block, preferred_element_type=jnp.float32)]
    ppermute x0 -> x20, starting transfers between devices: none -> 23.4 us  [the longest x6 7.93 us: on_device(): to_ends = lambda v: lax.ppermute(v, 'tensor', [(1, 0), (2, 3)])]
  transfers between devices with their start and end apart: 2 -> 20, of which waited for: 2 -> 8; matrix products, arithmetic and copies ran while one was open for 9% -> 0% of each run, Pallas kernels for 0% -> 47%
where the time goes in v1:
time: 209 us; the launch traced here: 208 us
  Pallas kernels  99.7 us (48%)
  waiting for transfers between devices  80.6 us (39%)
  starting transfers between devices  23.4 us (11%)
  local copies, waits for them, and re-layouts  3.06 us (1%)
    ppermute x6, waiting for transfers between devices, on_device(): to_ends = lambda v: lax.ppermute(v, 'tensor', [(1, 0), (2, 3)])  74.5 us
    pallas_call x3, Pallas kernels, hidden_grad(): pl.pallas_call(functools.partial(hidden_grad_kernel, half, tuple((len(s)...  33.3 us
    pallas_call x2, Pallas kernels, weight_grad(): pl.pallas_call(functools.partial(weight_grad_kernel, len(hiddens)), grid=...  28.3 us
    pallas_call x2, Pallas kernels, factors(): pl.pallas_call(kernel, grid=(tok // rows,), in_specs=[spec(columns)] * 2,...  20.6 us
    pallas_call x1, Pallas kernels, load_weight(): pl.pallas_call(load_weight_kernel, in_specs=[ANY_SPEC], out_specs=[VMEM_S...  9.98 us
    ppermute x6, starting transfers between devices, on_device(): to_ends = lambda v: lax.ppermute(v, 'tensor', [(1, 0), (2, 3)])  7.93 us
    ppermute x3, starting transfers between devices, on_device(): swap_pair = lambda v: lax.ppermute(v, 'tensor', both_ways((0, 1), (2, 3)))  5.92 us
    pallas_call x2, Pallas kernels, add_rows(): pl.pallas_call(functools.partial(add_kernel, scale), grid=(rows // tile,)...  5.51 us
  transfers between devices with their start and end apart: 20, of which 8 were waited for; matrix products, arithmetic and copies ran while one was open for 0% of the time, Pallas kernels for 47%

profile of v1, /device:TPU:0, one launch (start us, length us, event | category | flops | bytes accessed | tf_op | source)
XLA Modules:
  0.0 207.8 jit_solution(18155384315555431253)
XLA Ops:
  0.7 1.4 dynamic-slice_bitcast_fusion
  2.1 3.0 %collective-permute-start = (bf16[160,2048]{1,0:T(8,128)(2,1)S(1)}, bf16[160,2048]{1,0:T(8,128)(2,1)S(1)}, u32[]{:S(2)}, u32[]{:S(2)}) collective-permute-start(bf16[160,2048]{1,0:T(8,128)(2,1)S(1)} %get-tuple-element.64.refs_2_), channel_id=1, source_target_pairs={{0,2},{1,3},{2,0},{3,1},{4,6},{5,7},{6,4},{7,5},{8,10},{9,11},{10,... | collective-permute-start | bytes 1966088 | tf_op jit(solution)/shard_map/ppermute | solution.py:319
  5.1 1.6 collective-permute-start.3
  6.7 0.7 collective-permute-start.4
  7.4 8.4 %factors.2.refs_0_ = bf16[640,2560]{1,0:T(8,128)(2,1)} custom-call(bf16[640,3584]{1,0:T(8,128)(2,1)} %bitcast.10, bf16[640,3584]{1,0:T(8,128)(2,1)} %bitcast.12), custom_call_target="tpu_custom_call" | custom-call | flops 32768000 | bytes 9830400 | tf_op jit(solution)/shard_map/factors/pallas_call | solution.py:148
  15.8 4.0 %collective-permute-done.refs_0_ = bf16[160,2048]{1,0:T(8,128)(2,1)S(1)} collective-permute-done((bf16[160,2048]{1,0:T(8,128)(2,1)S(1)}, bf16[160,2048]{1,0:T(8,128)(2,1)S(1)}, u32[]{:S(2)}, u32[]{:S(2)}) %collective-permute-start) | collective-permute-done | bytes 655392 | tf_op jit(solution)/shard_map/ppermute | solution.py:319
  19.8 1.7 collective-permute-start.13
  21.6 0.0 collective-permute-done.3.refs_1_
  21.6 0.0 collective-permute-done.4.refs_0_.refs_2_
  21.6 4.3 %collective-permute-start.5 = (bf16[160,2048]{1,0:T(8,128)(2,1)S(1)}, bf16[160,2048]{1,0:T(8,128)(2,1)S(1)}, u32[]{:S(2)}, u32[]{:S(2)}) collective-permute-start(bf16[160,2048]{1,0:T(8,128)(2,1)S(1)} %get-tuple-element.64.refs_2_), channel_id=1, source_target_pairs={{0,4},{4,0},{8,12},{12,8},{1,5},{5,1},{9,13},{13,9},{2,6},{6,2},{1... | collective-permute-start | bytes 1966088 | tf_op jit(solution)/shard_map/ppermute | solution.py:332
  25.9 0.0 collective-permute-start.1
  25.9 0.7 collective-permute-start.2
  26.6 0.7 collective-permute-start.11
  27.3 12.1 %factors.3 = (bf16[640,1024]{1,0:T(8,128)(2,1)}, bf16[640,3584]{1,0:T(8,128)(2,1)}, bf16[640,3584]{1,0:T(8,128)(2,1)}) custom-call(bf16[640,3584]{1,0:T(8,128)(2,1)} %bitcast.11, bf16[640,3584]{1,0:T(8,128)(2,1)} %bitcast.13), custom_call_target="tpu_custom_call" | custom-call | flops 45875200 | bytes 19660800 | tf_op jit(solution)/shard_map/factors/pallas_call | solution.py:148
  39.5 2.1 collective-permute-done.5.refs_3_
  41.5 0.7 collective-permute-start.9
  42.2 10.0 %load_weight.1 = (bf16[3584,2048]{1,0:T(8,128)(2,1)S(1)}, bf16[3584,2048]{1,0:T(8,128)(2,1)S(1)}, f32[8,128]{1,0:T(8,128)}) custom-call(bf16[3584,4096]{1,0:T(8,128)(2,1)} %weight), custom_call_target="tpu_custom_call" | custom-call | bytes 58720256 | tf_op jit(solution)/shard_map/load_weight/pallas_call | solution.py:118
  52.2 0.0 copy-start.2
  52.2 15.4 %hidden_grad_early.1 = (bf16[640,3584]{1,0:T(8,128)(2,1)}, bf16[640,3584]{1,0:T(8,128)(2,1)}) custom-call(bf16[160,2048]{1,0:T(8,128)(2,1)S(1)} %get-tuple-element.62.refs_0_, bf16[160,2048]{1,0:T(8,128)(2,1)S(1)} %collective-permute-done.3.refs_1_, bf16[160,2048]{1,0:T(8,128)(2,1)S(1)} %get-tuple-element.64.refs_2_, ...), custom_call_target="tpu_custom_call" | custom-call | flops 9395240960 | bytes 13762560 | tf_op jit(solution)/shard_map/hidden_grad_early/pallas_call | solution.py:228
  67.6 0.0 collective-permute-done.1.refs_1_
  67.7 1.3 collective-permute-start.8
  69.0 0.0 collective-permute-done.2.refs_2_
  69.0 0.7 collective-permute-start.7
  69.7 0.0 collective-permute-done.9.refs_1_.refs_3_
  69.7 1.3 collective-permute-start.10
  71.0 0.0 collective-permute-done.11.refs_0_
  71.0 20.9 %collective-permute-done.8.refs_2_.refs_4_ = bf16[160,2048]{1,0:T(8,128)(2,1)S(1)} collective-permute-done((bf16[160,2048]{1,0:T(8,128)(2,1)S(1)}, bf16[160,2048]{1,0:T(8,128)(2,1)S(1)}, u32[]{:S(2)}, u32[]{:S(2)}) %collective-permute-start.8) | collective-permute-done | bytes 655392 | tf_op jit(solution)/shard_map/ppermute | solution.py:334
  91.9 0.0 collective-permute-done.7.refs_3_
  91.9 10.2 %collective-permute-done.10.refs_3_.refs_5_ = bf16[160,2048]{1,0:T(8,128)(2,1)S(1)} collective-permute-done((bf16[160,2048]{1,0:T(8,128)(2,1)S(1)}, bf16[160,2048]{1,0:T(8,128)(2,1)S(1)}, u32[]{:S(2)}, u32[]{:S(2)}) %collective-permute-start.10) | collective-permute-done | bytes 655392 | tf_op jit(solution)/shard_map/ppermute | solution.py:334
  102.1 0.7 collective-permute-start.14
  102.8 1.3 collective-permute-start.6
  104.1 1.3 collective-permute-start.12
  105.4 0.0 copy-done.2
  105.5 0.6 collective-permute-start.15
  106.0 7.8 %hidden_grad_late_partial.1.refs_5_ = f32[320,3584]{1,0:T(8,128)} custom-call(bf16[160,2048]{1,0:T(8,128)(2,1)S(1)} %collective-permute-done.4.refs_0_.refs_2_, bf16[160,2048]{1,0:T(8,128)(2,1)S(1)} %collective-permute-done.9.refs_1_.refs_3_, bf16[160,2048]{1,0:T(8,128)(2,1)S(1)} %collective-permute-done.8.refs_2_.refs_4_, ...), custom_call_target="tpu_custom_call" | custom-call | flops 4697620480 | bytes 13762560 | tf_op jit(solution)/shard_map/hidden_grad_late_partial/pallas_call | solution.py:228
  113.8 0.9 in_token_order.2.refs_6_
  114.7 0.0 collective-permute-done.14.refs_1_
  114.7 7.7 %collective-permute-done.6.refs_4_ = bf16[160,2048]{1,0:T(8,128)(2,1)S(1)} collective-permute-done((bf16[160,2048]{1,0:T(8,128)(2,1)S(1)}, bf16[160,2048]{1,0:T(8,128)(2,1)S(1)}, u32[]{:S(2)}, u32[]{:S(2)}) %collective-permute-start.6) | collective-permute-done | bytes 655392 | tf_op jit(solution)/shard_map/ppermute | solution.py:334
  122.4 9.3 %collective-permute-done.12.refs_5_ = bf16[160,2048]{1,0:T(8,128)(2,1)S(1)} collective-permute-done((bf16[160,2048]{1,0:T(8,128)(2,1)S(1)}, bf16[160,2048]{1,0:T(8,128)(2,1)S(1)}, u32[]{:S(2)}, u32[]{:S(2)}) %collective-permute-start.12) | collective-permute-done | bytes 655392 | tf_op jit(solution)/shard_map/ppermute | solution.py:334
  131.7 0.0 collective-permute-done.13.refs_1_
  131.7 0.0 copy-start.1
  131.7 1.1 in_token_order.3.refs_2_
  132.8 0.6 copy-done.1
  133.4 18.8 %weight_grad.2 = (bf16[2560,1024]{1,0:T(8,128)(2,1)}, bf16[2560,1024]{1,0:T(8,128)(2,1)}) custom-call(bf16[640,2560]{1,0:T(8,128)(2,1)} %factors.2.refs_0_, bf16[640,2560]{1,0:T(8,128)(2,1)} %copy-done.1, bf16[1280,2048]{1,0:T(8,128)(2,1)S(1)} %in_token_order.3.refs_2_), custom_call_target="tpu_custom_call" | custom-call | flops 13421772800 | bytes 17039360 | tf_op jit(solution)/shard_map/weight_grad/pallas_call | solution.py:267
  152.2 0.0 collective-permute-done.15.refs_1_
  152.2 0.0 copy-start.3
  152.2 0.0 slice-start
  152.2 0.0 slice-start.1
  152.2 0.1 collective-permute-start.16
  152.3 1.0 copy-done.3
  153.3 9.6 %weight_grad.3 = (bf16[1024,1024]{1,0:T(8,128)(2,1)}, bf16[1024,1024]{1,0:T(8,128)(2,1)}) custom-call(bf16[640,1024]{1,0:T(8,128)(2,1)} %get-tuple-element.92.refs_0_, bf16[640,1024]{1,0:T(8,128)(2,1)} %copy-done.3, bf16[1280,2048]{1,0:T(8,128)(2,1)S(1)} %in_token_order.3.refs_2_), custom_call_target="tpu_custom_call" | custom-call | flops 5368709120 | bytes 6815744 | tf_op jit(solution)/shard_map/weight_grad/pallas_call | solution.py:267
  162.8 0.0 collective-permute-done.16.b_ref
  162.9 0.0 collective-permute-start.17
  162.9 1.3 collective-permute-start.18
  164.2 1.5 collective-permute-start.19
  165.6 0.0 slice-done
  165.7 0.0 slice-done.1
  165.7 3.9 %add_rows.2.refs_0_ = bf16[3584,1024]{1,0:T(8,128)(2,1)} custom-call(bf16[2560,1024]{1,0:T(8,128)(2,1)S(1)} %bitcast.9, bf16[2560,1024]{1,0:T(8,128)(2,1)S(1)} %collective-permute-done.16.b_ref), custom_call_target="tpu_custom_call" | custom-call | flops 5242880 | bytes 15728640 | tf_op jit(solution)/shard_map/add_rows/pallas_call | solution.py:295
  169.5 12.8 %collective-permute-done.18.refs_2_ = bf16[160,2048]{1,0:T(8,128)(2,1)S(1)} collective-permute-done((bf16[160,2048]{1,0:T(8,128)(2,1)S(1)}, bf16[160,2048]{1,0:T(8,128)(2,1)S(1)}, u32[]{:S(2)}, u32[]{:S(2)}) %collective-permute-start.18) | collective-permute-done | bytes 655392 | tf_op jit(solution)/shard_map/ppermute | solution.py:334
  182.3 13.6 %collective-permute-done.19.refs_3_ = bf16[160,2048]{1,0:T(8,128)(2,1)S(1)} collective-permute-done((bf16[160,2048]{1,0:T(8,128)(2,1)S(1)}, bf16[160,2048]{1,0:T(8,128)(2,1)S(1)}, u32[]{:S(2)}, u32[]{:S(2)}) %collective-permute-start.19) | collective-permute-done | bytes 655392 | tf_op jit(solution)/shard_map/ppermute | solution.py:334
  195.9 10.2 %hidden_grad_late.1 = (bf16[640,3584]{1,0:T(8,128)(2,1)}, bf16[640,3584]{1,0:T(8,128)(2,1)}) custom-call(bf16[160,2048]{1,0:T(8,128)(2,1)S(1)} %collective-permute-done.11.refs_0_, bf16[160,2048]{1,0:T(8,128)(2,1)S(1)} %collective-permute-done.14.refs_1_, ...), custom_call_target="tpu_custom_call", output_to_operand_aliasing={{0}: (8, {}), {1}: (9, {})} | custom-call | flops 4697620480 | bytes 13762560 | tf_op jit(solution)/shard_map/hidden_grad_late/pallas_call | solution.py:228
  206.1 0.0 collective-permute-done.17.b_ref
  206.1 0.0 copy-done
  206.1 1.7 add_rows.3
  (2 shorter events, 0.0 us)
Async XLA Ops:
  2.1 17.7 %collective-permute-start = (bf16[160,2048]{1,0:T(8,128)(2,1)S(1)}, bf16[160,2048]{1,0:T(8,128)(2,1)S(1)}, u32[]{:S(2)}, u32[]{:S(2)}) collective-permute-start(bf16[160,2048]{1,0:T(8,128)(2,1)S(1)} %get-tuple-element.64.refs_2_), channel_id=1, source_target_pairs={{0,2},{1,3},{2,0},{3,1},{4,6},{5,7},{6,4},{7,5},{8,10},{9,11},{10,... | collective-permute-start | bytes 1966088 | tf_op jit(solution)/shard_map/ppermute | solution.py:319
  5.1 16.5 %collective-permute-start.3 = (bf16[160,2048]{1,0:T(8,128)(2,1)S(1)}, bf16[160,2048]{1,0:T(8,128)(2,1)S(1)}, u32[]{:S(2)}, u32[]{:S(2)}) collective-permute-start(bf16[160,2048]{1,0:T(8,128)(2,1)S(1)} %get-tuple-element.62.refs_0_), channel_id=1, source_target_pairs={{0,4},{4,0},{8,12},{12,8},{1,5},{5,1},{9,13},{13,9},{2,6},{6,2},{1... | collective-permute-start | bytes 1966088 | tf_op jit(solution)/shard_map/ppermute | solution.py:332
  6.7 14.9 %collective-permute-start.4 = (bf16[160,2048]{1,0:T(8,128)(2,1)S(1)}, bf16[160,2048]{1,0:T(8,128)(2,1)S(1)}, u32[]{:S(2)}, u32[]{:S(2)}) collective-permute-start(bf16[160,2048]{1,0:T(8,128)(2,1)S(1)} %get-tuple-element.62.refs_0_), channel_id=1, source_target_pairs={{4,8},{8,4},{5,9},{9,5},{6,10},{10,6},{7,11},{11,7},{20,24},{24,20... | collective-permute-start | bytes 1966088 | tf_op jit(solution)/shard_map/ppermute | solution.py:333
  19.8 111.9 %collective-permute-start.13 = (bf16[640,2560]{1,0:T(8,128)(2,1)}, bf16[640,2560]{1,0:T(8,128)(2,1)S(1)}, u32[]{:S(2)}, u32[]{:S(2)}) collective-permute-start(bf16[640,2560]{1,0:T(8,128)(2,1)} %factors.2.refs_0_), channel_id=1, source_target_pairs={{0,2},{1,3},{2,0},{3,1},{4,6},{5,7},{6,4},{7,5},{8,10},{9,11},{10,... | collective-permute-start | bytes 9830408 | tf_op jit(solution)/shard_map/ppermute | solution.py:319
  21.6 20.0 %collective-permute-start.5 = (bf16[160,2048]{1,0:T(8,128)(2,1)S(1)}, bf16[160,2048]{1,0:T(8,128)(2,1)S(1)}, u32[]{:S(2)}, u32[]{:S(2)}) collective-permute-start(bf16[160,2048]{1,0:T(8,128)(2,1)S(1)} %get-tuple-element.64.refs_2_), channel_id=1, source_target_pairs={{0,4},{4,0},{8,12},{12,8},{1,5},{5,1},{9,13},{13,9},{2,6},{6,2},{1... | collective-permute-start | bytes 1966088 | tf_op jit(solution)/shard_map/ppermute | solution.py:332
  25.9 41.8 %collective-permute-start.1 = (bf16[160,2048]{1,0:T(8,128)(2,1)S(1)}, bf16[160,2048]{1,0:T(8,128)(2,1)S(1)}, u32[]{:S(2)}, u32[]{:S(2)}) collective-permute-start(bf16[160,2048]{1,0:T(8,128)(2,1)S(1)} %collective-permute-done.refs_0_), channel_id=1, source_target_pairs={{0,4},{4,0},{8,12},{12,8},{1,5},{5,1},{9,13},{13,9},{2,6},{6,2},{1... | collective-permute-start | bytes 1966088 | tf_op jit(solution)/shard_map/ppermute | solution.py:332
  25.9 43.0 %collective-permute-start.2 = (bf16[160,2048]{1,0:T(8,128)(2,1)S(1)}, bf16[160,2048]{1,0:T(8,128)(2,1)S(1)}, u32[]{:S(2)}, u32[]{:S(2)}) collective-permute-start(bf16[160,2048]{1,0:T(8,128)(2,1)S(1)} %collective-permute-done.refs_0_), channel_id=1, source_target_pairs={{4,8},{8,4},{5,9},{9,5},{6,10},{10,6},{7,11},{11,7},{20,24},{24,20... | collective-permute-start | bytes 1966088 | tf_op jit(solution)/shard_map/ppermute | solution.py:333
  26.6 44.4 %collective-permute-start.11 = (bf16[160,2048]{1,0:T(8,128)(2,1)S(1)}, bf16[160,2048]{1,0:T(8,128)(2,1)S(1)}, u32[]{:S(2)}, u32[]{:S(2)}) collective-permute-start(bf16[160,2048]{1,0:T(8,128)(2,1)S(1)} %get-tuple-element.64.refs_2_), channel_id=1, source_target_pairs={{4,8},{8,4},{5,9},{9,5},{6,10},{10,6},{7,11},{11,7},{20,24},{24,20... | collective-permute-start | bytes 1966088 | tf_op jit(solution)/shard_map/ppermute | solution.py:333
  41.5 28.1 %collective-permute-start.9 = (bf16[160,2048]{1,0:T(8,128)(2,1)S(1)}, bf16[160,2048]{1,0:T(8,128)(2,1)S(1)}, u32[]{:S(2)}, u32[]{:S(2)}) collective-permute-start(bf16[160,2048]{1,0:T(8,128)(2,1)S(1)} %collective-permute-done.3.refs_1_), channel_id=1, source_target_pairs={{4,8},{8,4},{5,9},{9,5},{6,10},{10,6},{7,11},{11,7},{20,24},{24,20... | collective-permute-start | bytes 1966088 | tf_op jit(solution)/shard_map/ppermute | solution.py:333
  52.2 53.2 %copy-start.2 = (bf16[640,1024]{1,0:T(8,128)(2,1)S(1)}, bf16[640,1024]{1,0:T(8,128)(2,1)}, u32[]{:S(2)}) copy-start(bf16[640,1024]{1,0:T(8,128)(2,1)} %get-tuple-element.92.refs_0_) | copy-start | bytes 3932164
  67.7 24.3 %collective-permute-start.8 = (bf16[160,2048]{1,0:T(8,128)(2,1)S(1)}, bf16[160,2048]{1,0:T(8,128)(2,1)S(1)}, u32[]{:S(2)}, u32[]{:S(2)}) collective-permute-start(bf16[160,2048]{1,0:T(8,128)(2,1)S(1)} %collective-permute-done.4.refs_0_.refs_2_), channel_id=1, source_target_pairs={{4,0},{8,12},{5,1},{9,13},{6,2},{10,14},{7,3},{11,15},{20,16},{24,... | collective-permute-start | bytes 1966088 | tf_op jit(solution)/shard_map/ppermute | solution.py:334
  69.0 22.9 %collective-permute-start.7 = (bf16[160,2048]{1,0:T(8,128)(2,1)S(1)}, bf16[160,2048]{1,0:T(8,128)(2,1)S(1)}, u32[]{:S(2)}, u32[]{:S(2)}) collective-permute-start(bf16[160,2048]{1,0:T(8,128)(2,1)S(1)} %collective-permute-done.1.refs_1_), channel_id=1, source_target_pairs={{4,8},{8,4},{5,9},{9,5},{6,10},{10,6},{7,11},{11,7},{20,24},{24,20... | collective-permute-start | bytes 1966088 | tf_op jit(solution)/shard_map/ppermute | solution.py:333
  69.7 32.5 %collective-permute-start.10 = (bf16[160,2048]{1,0:T(8,128)(2,1)S(1)}, bf16[160,2048]{1,0:T(8,128)(2,1)S(1)}, u32[]{:S(2)}, u32[]{:S(2)}) collective-permute-start(bf16[160,2048]{1,0:T(8,128)(2,1)S(1)} %collective-permute-done.9.refs_1_.refs_3_), channel_id=1, source_target_pairs={{4,0},{8,12},{5,1},{9,13},{6,2},{10,14},{7,3},{11,15},{20,16},{24,... | collective-permute-start | bytes 1966088 | tf_op jit(solution)/shard_map/ppermute | solution.py:334
  102.1 12.6 %collective-permute-start.14 = (bf16[160,2048]{1,0:T(8,128)(2,1)S(1)}, bf16[160,2048]{1,0:T(8,128)(2,1)S(1)}, u32[]{:S(2)}, u32[]{:S(2)}) collective-permute-start(bf16[160,2048]{1,0:T(8,128)(2,1)S(1)} %collective-permute-done.5.refs_3_), channel_id=1, source_target_pairs={{4,8},{8,4},{5,9},{9,5},{6,10},{10,6},{7,11},{11,7},{20,24},{24,20... | collective-permute-start | bytes 1966088 | tf_op jit(solution)/shard_map/ppermute | solution.py:333
  102.8 19.6 %collective-permute-start.6 = (bf16[160,2048]{1,0:T(8,128)(2,1)S(1)}, bf16[160,2048]{1,0:T(8,128)(2,1)S(1)}, u32[]{:S(2)}, u32[]{:S(2)}) collective-permute-start(bf16[160,2048]{1,0:T(8,128)(2,1)S(1)} %collective-permute-done.2.refs_2_), channel_id=1, source_target_pairs={{4,0},{8,12},{5,1},{9,13},{6,2},{10,14},{7,3},{11,15},{20,16},{24,... | collective-permute-start | bytes 1966088 | tf_op jit(solution)/shard_map/ppermute | solution.py:334
  104.1 27.6 %collective-permute-start.12 = (bf16[160,2048]{1,0:T(8,128)(2,1)S(1)}, bf16[160,2048]{1,0:T(8,128)(2,1)S(1)}, u32[]{:S(2)}, u32[]{:S(2)}) collective-permute-start(bf16[160,2048]{1,0:T(8,128)(2,1)S(1)} %collective-permute-done.7.refs_3_), channel_id=1, source_target_pairs={{4,0},{8,12},{5,1},{9,13},{6,2},{10,14},{7,3},{11,15},{20,16},{24,... | collective-permute-start | bytes 1966088 | tf_op jit(solution)/shard_map/ppermute | solution.py:334
  105.5 46.8 %collective-permute-start.15 = (bf16[640,1024]{1,0:T(8,128)(2,1)S(1)}, bf16[640,1024]{1,0:T(8,128)(2,1)S(1)}, u32[]{:S(2)}, u32[]{:S(2)}) collective-permute-start(bf16[640,1024]{1,0:T(8,128)(2,1)S(1)} %copy-done.2), channel_id=1, source_target_pairs={{0,2},{1,3},{2,0},{3,1},{4,6},{5,7},{6,4},{7,5},{8,10},{9,11},{10,... | collective-permute-start | bytes 3932168 | tf_op jit(solution)/shard_map/ppermute | solution.py:319
  131.7 1.7 copy-start.1
  152.2 1.1 copy-start.3
  152.2 13.4 %slice-start = ((s8[5242880]{0:T(1024)(128)(4,1)}), s8[4194304]{0:T(1024)(128)(4,1)S(1)}, s32[]{:S(2)}) async-start(s8[5242880]{0:T(1024)(128)(4,1)} %bitcast.8), calls=%async_computation | async-start | bytes 8388608
  152.2 13.4 %slice-start.1 = ((s8[5242880]{0:T(1024)(128)(4,1)}), s8[1048576]{0:T(1024)(128)(4,1)S(1)}, s32[]{:S(2)}) async-start(s8[5242880]{0:T(1024)(128)(4,1)} %bitcast.8), calls=%async_computation.1 | async-start | bytes 2097152
  152.2 10.6 %collective-permute-start.16 = (bf16[2560,1024]{1,0:T(8,128)(2,1)}, bf16[2560,1024]{1,0:T(8,128)(2,1)S(1)}, u32[]{:S(2)}, u32[]{:S(2)}) collective-permute-start(bf16[2560,1024]{1,0:T(8,128)(2,1)} %get-tuple-element.96), channel_id=1, source_target_pairs={{0,1},{1,0},{2,3},{3,2},{4,5},{5,4},{6,7},{7,6},{8,9},{9,8},{10,11... | collective-permute-start | bytes 15728648 | tf_op jit(solution)/shard_map/ppermute | solution.py:324
  162.9 43.2 %collective-permute-start.17 = (bf16[1024,1024]{1,0:T(8,128)(2,1)}, bf16[1024,1024]{1,0:T(8,128)(2,1)S(1)}, u32[]{:S(2)}, u32[]{:S(2)}) collective-permute-start(bf16[1024,1024]{1,0:T(8,128)(2,1)} %get-tuple-element.97), channel_id=1, source_target_pairs={{0,1},{1,0},{2,3},{3,2},{4,5},{5,4},{6,7},{7,6},{8,9},{9,8},{10,11... | collective-permute-start | bytes 6291464 | tf_op jit(solution)/shard_map/ppermute | solution.py:324
  162.9 19.4 %collective-permute-start.18 = (bf16[160,2048]{1,0:T(8,128)(2,1)S(1)}, bf16[160,2048]{1,0:T(8,128)(2,1)S(1)}, u32[]{:S(2)}, u32[]{:S(2)}) collective-permute-start(bf16[160,2048]{1,0:T(8,128)(2,1)S(1)} %collective-permute-done.11.refs_0_), channel_id=1, source_target_pairs={{4,0},{8,12},{5,1},{9,13},{6,2},{10,14},{7,3},{11,15},{20,16},{24,... | collective-permute-start | bytes 1966088 | tf_op jit(solution)/shard_map/ppermute | solution.py:334
  164.2 31.8 %collective-permute-start.19 = (bf16[160,2048]{1,0:T(8,128)(2,1)S(1)}, bf16[160,2048]{1,0:T(8,128)(2,1)S(1)}, u32[]{:S(2)}, u32[]{:S(2)}) collective-permute-start(bf16[160,2048]{1,0:T(8,128)(2,1)S(1)} %collective-permute-done.14.refs_1_), channel_id=1, source_target_pairs={{4,0},{8,12},{5,1},{9,13},{6,2},{10,14},{7,3},{11,15},{20,16},{24,... | collective-permute-start | bytes 1966088 | tf_op jit(solution)/shard_map/ppermute | solution.py:334
  169.5 36.6 %copy-start = (bf16[1024,1024]{1,0:T(8,128)(2,1)S(1)}, bf16[1024,1024]{1,0:T(8,128)(2,1)}, u32[]{:S(2)}) copy-start(bf16[1024,1024]{1,0:T(8,128)(2,1)} %get-tuple-element.112.a_ref) | copy-start | bytes 6291460

commit v2 on v1

v2 whole, which is shorter than its diff:
```python
import functools
import math

import jax
import jax.numpy as jnp
from jax import lax
from jax.experimental import pallas as pl
from jax.experimental.pallas import tpu as pltpu
from jax.sharding import PartitionSpec as P

VMEM_LIMIT = 10 * 1024 * 1024
F32, BF16 = jnp.float32, jnp.bfloat16
SHORT = pl.CostEstimate(flops=1, bytes_accessed=1, transcendentals=0)
LONG = pl.CostEstimate(flops=10**12, bytes_accessed=10**9, transcendentals=0)
ANY_SPEC = pl.BlockSpec(memory_space=pl.ANY)
VMEM_SPEC = pl.BlockSpec(memory_space=pltpu.VMEM)


def pick_tile(extent, cap):
    return max(t for t in range(128, cap + 1, 128) if extent % t == 0)


def together(*values):
    return lax.optimization_barrier(values)


def sigmoid(x):
    return 0.5 + 0.5 * jnp.tanh(0.5 * x)


def contract_last(a, b):
    return lax.dot_general(a, b, (((1,), (1,)), ((), ())), preferred_element_type=F32)


def contract_first(a, b):
    return lax.dot_general(a, b, (((0,), (0,)), ((), ())), preferred_element_type=F32)


def in_vmem(value):
    return pltpu.with_memory_space_constraint(value, pltpu.VMEM)


def in_hbm(values):
    return [pltpu.with_memory_space_constraint(v, pltpu.HBM) for v in values]


def place_shards(parts, half, into, sem, start, by_core=False):
    act = (lambda c: c.start()) if start else (lambda c: c.wait())
    z = lax.axis_index("tensor")
    pair = z // 2
    parts = list(parts)
    slot = iter(range(16))

    def place(ref, row):
        rows = ref.shape[0]
        at = pl.ds(pl.multiple_of(row, 16), rows)
        if not by_core:
            act(pltpu.make_async_copy(ref, into.at[at], sem.at[next(slot)]))
            return
        cols = ref.shape[1] // 2
        for k in range(2):
            there = pl.multiple_of(jnp.where(lax.axis_index("dp") % 2 == k, 1, 0) * cols, cols)
            copy = pltpu.make_async_copy(
                ref.at[:, pl.ds(k * cols, cols)], into.at[at, pl.ds(there, cols)], sem.at[next(slot)]
            )
            act(copy)

    if half != "late":
        whole = parts[0].shape[0] * (2 if half == "early" else 4) == into.shape[0]
        base = 0 if half == "early" else pair * (into.shape[0] // 2)
        if whole:
            rows = parts[0].shape[0]
            place(parts.pop(0), base + (z % 2) * rows)
            place(parts.pop(0), base + (1 - z % 2) * rows)
        else:
            place(parts.pop(0), base)
    if half != "early":
        base = 0 if half == "late" else (1 - pair) * (into.shape[0] // 2)
        middle = jnp.logical_or(z == 1, z == 2)
        rows = parts[0].shape[0]
        steps = [base] if len(parts) == 2 else [base + pair * rows, base + (1 - pair) * rows]
        n = len(parts) // 2

        @pl.when(middle)
        def _():
            for ref, row in zip(parts[:n], steps):
                place(ref, row)

        @pl.when(jnp.logical_not(middle))
        def _():
            for ref, row in zip(parts[n:], steps):
                place(ref, row)


def move_kernel(half, by_core, n_parts, *refs):
    parts, (into, sem) = refs[:n_parts], refs[-2:]
    for start in (True, False):
        place_shards(parts, half, into, sem, start, by_core)


def in_token_order(half, rows, parts, by_core=False, wait_for=()):
    cols = parts[0].shape[1]
    return pl.pallas_call(
        functools.partial(move_kernel, half, by_core, len(parts)),
        in_specs=[ANY_SPEC] * (len(parts) + len(wait_for)),
        out_specs=VMEM_SPEC,
        out_shape=pltpu.VMEM((rows, cols), BF16),
        scratch_shapes=[pltpu.SemaphoreType.DMA((16,))],
        compiler_params=pltpu.CompilerParams(vmem_limit_bytes=VMEM_LIMIT),
        name="in_token_order",
    )(*parts, *wait_for)


def mark_kernel(*refs):
    out = refs[-1]
    out[...] = jnp.zeros(out.shape, out.dtype)


def mark_of(values, cost):
    return pl.pallas_call(
        mark_kernel,
        in_specs=[ANY_SPEC] * len(values),
        out_specs=VMEM_SPEC,
        out_shape=jax.ShapeDtypeStruct((8, 128), F32),
        cost_estimate=pl.CostEstimate(flops=1, bytes_accessed=cost, transcendentals=0),
        compiler_params=pltpu.CompilerParams(vmem_limit_bytes=VMEM_LIMIT),
        name="mark",
    )(*values)


def load_weight_kernel(weight, *refs):
    outs, mark, sem = refs[:-2], refs[-2], refs[-1]
    chip = lax.axis_index("dp") // 2
    copies = []
    for s, out in enumerate(outs):
        width = out.shape[1]
        at = pl.multiple_of(lax.rem(chip + s, len(outs)) * width, width)
        copies.append(pltpu.make_async_copy(weight.at[:, pl.ds(at, width)], out, sem.at[s]))
    for copy in copies:
        copy.start()
    mark[...] = jnp.zeros(mark.shape, mark.dtype)
    for copy in copies:
        copy.wait()


def load_weight(weight, blocks):
    ff, d = weight.shape
    return pl.pallas_call(
        load_weight_kernel,
        in_specs=[ANY_SPEC],
        out_specs=[VMEM_SPEC] * (blocks + 1),
        out_shape=[pltpu.VMEM((ff, d // blocks), BF16)] * blocks + [jax.ShapeDtypeStruct((8, 128), F32)],
        scratch_shapes=[pltpu.SemaphoreType.DMA((blocks,))],
        cost_estimate=LONG,
        compiler_params=pltpu.CompilerParams(vmem_limit_bytes=VMEM_LIMIT),
        name="load_weight",
    )(*in_hbm([weight]))


def hidden_kernel(gate_ref, up_ref, *hidden_refs):
    at = 0
    for ref in hidden_refs:
        columns = slice(at, at + ref.shape[1])
        gate, up = gate_ref[:, columns].astype(F32), up_ref[:, columns].astype(F32)
        ref[...] = (gate * sigmoid(gate) * up).astype(BF16)
        at += ref.shape[1]


def hidden_chunks(gate, up, widths):
    tok, ff = gate.shape
    rows = next(r for r in (64, 32, 16) if tok % r == 0)
    spec = lambda w: pl.BlockSpec((rows, w), lambda i: (i, 0))
    return pl.pallas_call(
        hidden_kernel,
        grid=(tok // rows,),
        in_specs=[spec(ff)] * 2,
        out_specs=[spec(w) for w in widths],
        out_shape=[pltpu.HBM((tok, w), BF16) for w in widths],
        cost_estimate=SHORT,
        compiler_params=pltpu.CompilerParams(vmem_limit_bytes=VMEM_LIMIT),
        name="hidden",
    )(*in_hbm([gate, up]))


def hidden_grad_kernel(half, counts, tile, has_partial, finish, *refs):
    refs = list(refs)
    streams = [[refs.pop(0) for _ in range(count)] for count in counts]
    weights = [refs.pop(0) for _ in counts]
    partial = refs.pop(0) if has_partial else None
    if sum(counts) == len(counts):
        lhs = [stream[0] for stream in streams]
    else:
        sem = refs.pop()
        lhs = refs[-len(counts) :]
        refs = refs[: -len(counts)]

        @pl.when(pl.program_id(0) == 0)
        def _():
            for start in (True, False):
                for s, parts in enumerate(streams):
                    place_shards(parts, half, lhs[s], sem.at[s], start)

    step = pl.program_id(0)
    at = pl.multiple_of(step * tile, tile)
    total = partial[...] if has_partial else None
    for left, weight in zip(lhs, weights):
        term = contract_last(left[...], weight[pl.ds(at, tile), :])
        total = term if total is None else total + term
    if not finish:
        refs[-1][...] = total
        return
    gate, up = refs[0][...].astype(F32), refs[1][...].astype(F32)
    gate_out, up_out = refs[-2:]
    sig = sigmoid(gate)
    gate_out[...] = (total * up * sig * (1.0 + gate * (1.0 - sig))).astype(BF16)
    up_out[...] = (total * (gate * sig)).astype(BF16)


def hidden_grad(half, streams, weights, tok, partial=None, by=None, outs=None, wait_for=()):
    ff = weights[0].shape[0]
    rows = tok if half == "all" else tok // 2
    tile = pick_tile(ff, 896 if by is None else 512)

    def place(i):
        pair = lax.axis_index("tensor") // 2
        return ({"all": 0, "early": pair, "late": 1 - pair}[half], i)

    block = pl.BlockSpec((rows, tile), place)
    part_block = pl.BlockSpec((rows, tile), lambda i: (0, i))
    if all(len(s) == 1 for s in streams):
        in_specs, args, scratch = [VMEM_SPEC] * len(streams), [in_vmem(s[0]) for s in streams], []
    else:
        args = [part for s in streams for part in s]
        in_specs = [ANY_SPEC] * len(args)
        scratch = [pltpu.VMEM((rows, w.shape[1]), BF16) for w in weights] + [
            pltpu.SemaphoreType.DMA((len(weights), 16))
        ]
    in_specs += [VMEM_SPEC] * len(weights)
    args += [in_vmem(w) for w in weights]
    aliases = {}
    if partial is not None:
        in_specs.append(part_block)
        args += in_hbm([partial])
    if by is not None:
        in_specs += [block] * 2
        args += in_hbm(by)
    in_specs += [ANY_SPEC] * len(wait_for)
    args += wait_for
    if by is not None:
        out_shape, out_specs = [pltpu.HBM((tok, ff), BF16)] * 2, [block] * 2
        if outs is not None:
            aliases = {len(args): 0, len(args) + 1: 1}
            in_specs += [ANY_SPEC] * 2
            args += in_hbm(outs)
    else:
        out_shape, out_specs = pltpu.HBM((rows, ff), F32), part_block
    return pl.pallas_call(
        functools.partial(
            hidden_grad_kernel,
            half,
            tuple(len(s) for s in streams),
            tile,
            partial is not None,
            by is not None,
        ),
        grid=(ff // tile,),
        in_specs=in_specs,
        out_specs=out_specs,
        scratch_shapes=scratch,
        out_shape=out_shape,
        input_output_aliases=aliases,
        cost_estimate=LONG if outs is not None else SHORT,
        compiler_params=pltpu.CompilerParams(vmem_limit_bytes=VMEM_LIMIT),
        name="hidden_grad_" + half + ("" if by is not None else "_partial"),
    )(*args)


def weight_grad_kernel(tile, has_start, split, hidden, block, *refs):
    at = pl.ds(pl.multiple_of(pl.program_id(0) * tile, tile), tile)
    total = contract_first(hidden[...], block[...])
    if has_start:
        total = total + refs[0][at, :].astype(F32)
    total = total.astype(BF16)
    if not split:
        refs[-1][at, :] = total
        return
    send, keep = refs[-2:]
    half = send.shape[1]
    send[...] = total[:, :half]
    keep[...] = total[:, half:]


def weight_grad(block, hidden, start=None, split=True):
    (tok, ff), cols = hidden.shape, block.shape[1]
    tile = pick_tile(ff, 256)
    in_specs = [pl.BlockSpec((tok, tile), lambda i: (0, i)), VMEM_SPEC]
    args = [hidden, in_vmem(block)]
    if start is not None:
        in_specs.append(VMEM_SPEC)
        args.append(in_vmem(start))
    if split:
        out_specs = [pl.BlockSpec((tile, cols // 2), lambda i: (i, 0))] * 2
        out_shape = [pltpu.HBM((ff, cols // 2), BF16), jax.ShapeDtypeStruct((ff, cols // 2), BF16)]
    else:
        out_specs, out_shape = VMEM_SPEC, pltpu.VMEM((ff, cols), BF16)
    return pl.pallas_call(
        functools.partial(weight_grad_kernel, tile, start is not None, split),
        grid=(ff // tile,),
        in_specs=in_specs,
        out_specs=out_specs,
        out_shape=out_shape,
        cost_estimate=SHORT,
        compiler_params=pltpu.CompilerParams(vmem_limit_bytes=VMEM_LIMIT),
        name="weight_grad",
    )(*args)


def add_kernel(scale, a_ref, b_ref, *refs):
    refs[-1][...] = ((a_ref[...].astype(F32) + b_ref[...].astype(F32)) * scale).astype(BF16)


def add_rows(keep, got, scale, row, total_rows, out=None):
    rows, cols = keep.shape
    tile = pick_tile(math.gcd(rows, row), 512)
    first = row // tile
    spec = pl.BlockSpec((tile, cols), lambda i: (i, 0))
    in_specs, args, aliases = [spec] * 2, [keep, got], {}
    if out is not None:
        aliases = {2: 0}
        in_specs.append(ANY_SPEC)
        args += in_hbm([out])
    return pl.pallas_call(
        functools.partial(add_kernel, scale),
        grid=(rows // tile,),
        in_specs=in_specs,
        out_specs=pl.BlockSpec((tile, cols), lambda i: (i + first, 0)),
        out_shape=pltpu.HBM((total_rows, cols), BF16),
        input_output_aliases=aliases,
        cost_estimate=SHORT,
        compiler_params=pltpu.CompilerParams(vmem_limit_bytes=VMEM_LIMIT),
        name="add_rows",
    )(*args)


def on_device(out_grad, gate_pre, up_pre, down_weight):
    grad, gate, up = out_grad[0], gate_pre[0], up_pre[0]
    tok, ff = gate.shape
    d = grad.shape[1]
    dp, nt = lax.axis_size("dp"), lax.axis_size("tensor")
    chips = dp // 2
    cols = d // chips
    chip, pair = lax.axis_index("dp") // 2, lax.axis_index("tensor") // 2
    scale = 1.0 / math.sqrt(tok * dp)

    def shift(value, s):
        return lax.ppermute(
            value, "dp", [(2 * c + k, 2 * ((c + s) % chips) + k) for c in range(chips) for k in range(2)]
        )

    def swap_cores(value):
        return lax.ppermute(value, "dp", [(k, k ^ 1) for k in range(dp)])

    def columns_of(which):
        return lax.dynamic_slice(grad, (0, which * cols), (grad.shape[0], cols))

    if nt == 4 and chips == 2 and ff % 896 == 0:
        cut = 6 * ff // 7
        both_ways = lambda *pairs: [q for a, b in pairs for q in ((a, b), (b, a))]
        swap_pair = lambda v: lax.ppermute(v, "tensor", both_ways((0, 1), (2, 3)))
        swap_middle = lambda v: lax.ppermute(v, "tensor", both_ways((1, 2)))
        to_ends = lambda v: lax.ppermute(v, "tensor", [(1, 0), (2, 3)])

        mine, rest = together(columns_of(chip), columns_of(1 - chip))
        far, a1 = shift(rest, 1), swap_pair(mine)
        h0, h1 = hidden_chunks(gate, up, [cut, ff - cut])
        far, h0 = together(far, h0)
        a1, rest, first, weight, h1 = together(a1, rest, mark_of([far], 10**6), down_weight, h1)

        h0_in = shift(h0, 1)
        a3, a2 = swap_pair(far), swap_pair(rest)
        pair1 = in_token_order("early", tok // 2, [mine, a1], wait_for=[first])
        b1 = swap_middle(pair1)
        *weights, mark = load_weight(weight, chips)
        a3, mark = together(a3, mark)

        pair3 = in_token_order("early", tok // 2, [far, a3], wait_for=[mark])
        b3 = swap_middle(pair3)
        b1, a2 = together(b1, a2)

        c1 = to_ends(b1)
        pair2 = in_token_order("early", tok // 2, [rest, a2])
        outs = hidden_grad("early", [[pair1], [pair2]], weights, tok, None, (gate, up))
        b3, c1, outs, pair2, h1 = together(b3, c1, outs, pair2, h1)

        c3, b2 = to_ends(b3), swap_middle(pair2)
        h1_in = shift(h1, 1)
        partial = hidden_grad("late", [[b1, c1]], weights[:1], tok)
        h0, h1, partial = together(h0, h1, partial)
        block = in_token_order("all", tok, [pair1, b1, c1], by_core=True)
        own0, own1 = weight_grad(block, h0, split=False), weight_grad(block, h1, split=False)
        first = mark_of([own0, own1], 1)
        b2, partial, first = together(b2, partial, first)

        c2 = to_ends(b2)
        c3, h0_in, partial, first = together(c3, h0_in, partial, first)
        block = in_token_order("all", tok, [pair3, b3, c3], by_core=True, wait_for=[first])
        send0, keep0 = weight_grad(block, h0_in, own0)
        got0 = swap_cores(send0)
        send0, h1_in = together(send0, h1_in)
        send1, keep1 = weight_grad(block, h1_in, own1)
        got1 = swap_cores(send1)
        c2, send1, partial = together(c2, send1, partial)
        outs = hidden_grad("late", [[b2, c2]], weights[1:], tok, partial, (gate, up), outs, [send1])
        got0, got1, outs = together(got0, got1, outs)
        down_grad = add_rows(keep0, got0, scale, 0, ff)
        down_grad = add_rows(keep1, got1, scale, cut, ff, down_grad)
    else:
        gather = lambda v: lax.all_gather(v, "tensor", axis=0, tiled=True)
        (hidden,) = hidden_chunks(gate, up, [ff])
        hiddens = [hidden] + [shift(hidden, s) for s in range(1, chips)]

        def by_core(value):
            return jnp.where(lax.axis_index("dp") % 2 == 0, jnp.roll(value, cols // 2, axis=1), value)

        blocks = [by_core(gather(columns_of(chip)))]
        blocks += [by_core(gather(shift(columns_of((chip + s) % chips), s))) for s in range(1, chips)]
        total = None
        for block, part in zip(blocks[:-1], hiddens[:-1]):
            total = weight_grad(block, part, total, split=False)
        send, keep = weight_grad(blocks[-1], hiddens[-1], total)
        outs = hidden_grad("all", [[gather(grad)]], load_weight(down_weight, 1)[:1], tok, None, (gate, up))
        down_grad = add_rows(keep, swap_cores(send), scale, 0, ff)
    return (outs[0][None], outs[1][None], down_grad)


def solution(mesh):
    return jax.shard_map(
        on_device,
        mesh=mesh,
        in_specs=(
            P("dp", ("groups", "tensor"), None),
            P("dp", "groups", "tensor"),
            P("dp", "groups", "tensor"),
            P("tensor", None),
        ),
        out_specs=(
            P("dp", "groups", "tensor"),
            P("dp", "groups", "tensor"),
            P(("groups", "tensor"), "dp"),
        ),
        check_vma=False,
    )
```

time: 209 us -> 169 us (0.81)
  waiting for transfers between devices: 80.6 us -> 44.9 us
  starting transfers between devices: 23.4 us -> 16.7 us
  Pallas kernels: 99.7 us -> 102 us
    ppermute x6 -> x3, waiting for transfers between devices: 74.5 us -> 30.1 us  [on_device(): to_ends = lambda v: lax.ppermute(v, 'tensor', [(1, 0), (2, 3)])]
    ppermute x3, waiting for transfers between devices: 2.07 us -> 10.6 us  [on_device(): swap_pair = lambda v: lax.ppermute(v, 'tensor', both_ways((0, 1), (2, 3)))]
    pallas_call x2, Pallas kernels: 5.51 us -> 9.97 us  [add_rows(): pl.pallas_call(functools.partial(add_kernel, scale), grid=(rows // tile,)...]
    ppermute x6 -> x3, starting transfers between devices: 7.93 us -> 3.87 us  [on_device(): to_ends = lambda v: lax.ppermute(v, 'tensor', [(1, 0), (2, 3)])]
    pallas_call x6 -> x12, Pallas kernels: 50.9 us -> 48.7 us  [the longest x4 32 us: weight_grad(): pl.pallas_call(functools.partial(weight_grad_kernel, tile, start is not N...]
  transfers between devices with their start and end apart: 20 -> 14, of which waited for: 8 -> 6; matrix products, arithmetic and copies ran while one was open for 0% -> 0% of each run, Pallas kernels for 47% -> 55%
where the time goes in v2:
time: 169 us; the launch traced here: 168 us
  Pallas kernels  102 us (60%)
  waiting for transfers between devices  44.9 us (27%)
  starting transfers between devices  16.7 us (10%)
  local copies, waits for them, and re-layouts  3.53 us (2%)
    pallas_call x3, Pallas kernels, hidden_grad(): pl.pallas_call(functools.partial(hidden_grad_kernel, half, tuple((len(s)...  33.8 us
    pallas_call x4, Pallas kernels, weight_grad(): pl.pallas_call(functools.partial(weight_grad_kernel, tile, start is not N...  32 us
    ppermute x3, waiting for transfers between devices, on_device(): to_ends = lambda v: lax.ppermute(v, 'tensor', [(1, 0), (2, 3)])  30.1 us
    ppermute x3, waiting for transfers between devices, on_device(): swap_pair = lambda v: lax.ppermute(v, 'tensor', both_ways((0, 1), (2, 3)))  10.6 us
    pallas_call x2, Pallas kernels, add_rows(): pl.pallas_call(functools.partial(add_kernel, scale), grid=(rows // tile,)...  9.97 us
    pallas_call x1, Pallas kernels, load_weight(): pl.pallas_call(load_weight_kernel, in_specs=[ANY_SPEC], out_specs=[VMEM_S...  9.37 us
    pallas_call x1, Pallas kernels, hidden_chunks(): pl.pallas_call(hidden_kernel, grid=(tok // rows,), in_specs=[spec(ff)] *...  9.3 us
    pallas_call x5, Pallas kernels, in_token_order(): pl.pallas_call(functools.partial(move_kernel, half, by_core, len(parts)),...  7.41 us
  transfers between devices with their start and end apart: 14, of which 6 were waited for; matrix products, arithmetic and copies ran while one was open for 0% of the time, Pallas kernels for 55%

profile of v2, /device:TPU:0, one launch (start us, length us, event | category | flops | bytes accessed | tf_op | source)
XLA Modules:
  0.0 167.9 jit_solution(14457335714590403602)
XLA Ops:
  0.7 2.3 %dynamic-slice_bitcast_fusion = (bf16[160,2048]{1,0:T(8,128)(2,1)}, bf16[160,2048]{1,0:T(8,128)(2,1)S(1)}) fusion(bf16[1,160,4096]{2,1,0:T(8,128)(2,1)} %param.4, s32[]{:T(128)S(6)} %select_n.13, s32[]{:T(128)S(6)} %select_n.12), kind=kLoop, calls=%fused_computation | loop fusion | bytes 2621448 | tf_op jit(solution)/shard_map/dynamic_slice | solution.py:364
  2.9 2.9 %collective-permute-start = (bf16[160,2048]{1,0:T(8,128)(2,1)}, bf16[160,2048]{1,0:T(8,128)(2,1)}, u32[]{:S(2)}, u32[]{:S(2)}) collective-permute-start(bf16[160,2048]{1,0:T(8,128)(2,1)} %get-tuple-element.64.refs_0_), channel_id=1, source_target_pairs={{0,2},{1,3},{2,0},{3,1},{4,6},{5,7},{6,4},{7,5},{8,10},{9,11},{10,... | collective-permute-start | bytes 1966088 | tf_op jit(solution)/shard_map/ppermute | solution.py:356
  5.9 1.6 collective-permute-start.2
  7.4 9.3 %hidden.1 = (bf16[640,3072]{1,0:T(8,128)(2,1)}, bf16[640,512]{1,0:T(8,128)(2,1)}) custom-call(bf16[640,3584]{1,0:T(8,128)(2,1)} %bitcast.10, bf16[640,3584]{1,0:T(8,128)(2,1)} %bitcast.13), custom_call_target="tpu_custom_call" | custom-call | flops 1 | bytes 1 | tf_op jit(solution)/shard_map/hidden/pallas_call | solution.py:173
  16.7 4.2 %collective-permute-done.refs_0_ = bf16[160,2048]{1,0:T(8,128)(2,1)} collective-permute-done((bf16[160,2048]{1,0:T(8,128)(2,1)}, bf16[160,2048]{1,0:T(8,128)(2,1)}, u32[]{:S(2)}, u32[]{:S(2)}) %collective-permute-start) | collective-permute-done | bytes 655392 | tf_op jit(solution)/shard_map/ppermute | solution.py:356
  20.9 1.8 %collective-permute-start.1 = (bf16[160,2048]{1,0:T(8,128)(2,1)}, bf16[160,2048]{1,0:T(8,128)(2,1)}, u32[]{:S(2)}, u32[]{:S(2)}) collective-permute-start(bf16[160,2048]{1,0:T(8,128)(2,1)} %collective-permute-done.refs_0_), channel_id=1, source_target_pairs={{0,4},{4,0},{8,12},{12,8},{1,5},{5,1},{9,13},{13,9},{2,6},{6,2},{1... | collective-permute-start | bytes 1966088 | tf_op jit(solution)/shard_map/ppermute | solution.py:369
  22.7 0.0 collective-permute-done.2.refs_1_
  22.7 0.9 collective-permute-start.5
  23.6 1.6 in_token_order.6.refs_0_
  25.3 1.7 %collective-permute-start.4 = (bf16[320,2048]{1,0:T(8,128)(2,1)}, bf16[320,2048]{1,0:T(8,128)(2,1)}, u32[]{:S(2)}, u32[]{:S(2)}) collective-permute-start(bf16[320,2048]{1,0:T(8,128)(2,1)} %in_token_order.6.refs_0_), channel_id=1, source_target_pairs={{4,8},{8,4},{5,9},{9,5},{6,10},{10,6},{7,11},{11,7},{20,24},{24,20... | collective-permute-start | bytes 3932168 | tf_op jit(solution)/shard_map/ppermute | solution.py:370
  27.0 1.1 collective-permute-start.8
  28.0 9.4 %load_weight.1 = (bf16[3584,2048]{1,0:T(8,128)(2,1)S(1)}, bf16[3584,2048]{1,0:T(8,128)(2,1)S(1)}, f32[8,128]{1,0:T(8,128)S(1)}) custom-call(bf16[3584,4096]{1,0:T(8,128)(2,1)} %weight), custom_call_target="tpu_custom_call" | custom-call | flops 999999995904 | bytes 1000000000 | tf_op jit(solution)/shard_map/load_weight/pallas_call | solution.py:148
  37.4 0.0 copy-start
  37.4 1.5 collective-permute-done.1.refs_1_
  38.9 2.4 %in_token_order.5.refs_0_ = bf16[320,2048]{1,0:T(8,128)(2,1)S(1)} custom-call(bf16[160,2048]{1,0:T(8,128)(2,1)} %collective-permute-done.refs_0_, bf16[160,2048]{1,0:T(8,128)(2,1)} %collective-permute-done.1.refs_1_, f32[8,128]{1,0:T(8,128)S(1)} %get-tuple-element.61.refs_2_), custom_call_target="tpu_custom_call" | custom-call | tf_op jit(solution)/shard_map/in_token_order/pallas_call | solution.py:103
  41.3 0.7 collective-permute-start.3
  42.1 9.1 %collective-permute-done.5.refs_1_ = bf16[160,2048]{1,0:T(8,128)(2,1)} collective-permute-done((bf16[160,2048]{1,0:T(8,128)(2,1)}, bf16[160,2048]{1,0:T(8,128)(2,1)}, u32[]{:S(2)}, u32[]{:S(2)}) %collective-permute-start.5) | collective-permute-done | bytes 655392 | tf_op jit(solution)/shard_map/ppermute | solution.py:369
  51.2 0.0 collective-permute-done.4.refs_0_.refs_1_
  51.2 1.3 collective-permute-start.6
  52.5 1.4 in_token_order.7.refs_1_
  53.9 15.0 %hidden_grad_early.1 = (bf16[640,3584]{1,0:T(8,128)(2,1)}, bf16[640,3584]{1,0:T(8,128)(2,1)}) custom-call(bf16[320,2048]{1,0:T(8,128)(2,1)} %in_token_order.6.refs_0_, bf16[320,2048]{1,0:T(8,128)(2,1)S(1)} %in_token_order.7.refs_1_, bf16[3584,2048]{1,0:T(8,128)(2,1)S(1)} %get-tuple-element.67.refs_2_, ...), custom_call_target="tpu_custom_call" | custom-call | flops 1 | bytes 1 | tf_op jit(solution)/shard_map/hidden_grad_early/pallas_call | solution.py:257
  68.9 0.0 copy-done
  68.9 0.0 collective-permute-done.3.refs_1_
  68.9 17.4 %collective-permute-done.6.refs_1_.refs_2_ = bf16[320,2048]{1,0:T(8,128)(2,1)S(1)} collective-permute-done((bf16[320,2048]{1,0:T(8,128)(2,1)}, bf16[320,2048]{1,0:T(8,128)(2,1)S(1)}, u32[]{:S(2)}, u32[]{:S(2)}) %collective-permute-start.6) | collective-permute-done | bytes 1310752 | tf_op jit(solution)/shard_map/ppermute | solution.py:371
  86.3 0.7 collective-permute-start.9
  87.0 1.3 collective-permute-start.7
  88.3 7.5 %hidden_grad_late_partial.1.refs_3_ = f32[320,3584]{1,0:T(8,128)} custom-call(bf16[320,2048]{1,0:T(8,128)(2,1)} %collective-permute-done.4.refs_0_.refs_1_, bf16[320,2048]{1,0:T(8,128)(2,1)S(1)} %collective-permute-done.6.refs_1_.refs_2_, bf16[3584,2048]{1,0:T(8,128)(2,1)S(1)} %get-tuple-element.67.refs_2_), custom_call_target="tpu_custom_call" | custom-call | flops 1 | bytes 1 | tf_op jit(solution)/shard_map/hidden_grad_late_partial/pallas_call | solution.py:257
  95.9 0.0 copy-start.2
  95.9 0.0 copy-start.1
  95.9 1.6 in_token_order.8.block
  97.5 0.0 copy-done.2
  97.5 2.1 %weight_grad.5.refs_1_.refs_0_ = bf16[512,2048]{1,0:T(8,128)(2,1)S(1)} custom-call(bf16[640,512]{1,0:T(8,128)(2,1)S(1)} %copy-done.2, bf16[640,2048]{1,0:T(8,128)(2,1)S(1)} %in_token_order.8.block), custom_call_target="tpu_custom_call" | custom-call | flops 1 | bytes 1 | tf_op jit(solution)/shard_map/weight_grad/pallas_call | solution.py:306
  99.6 0.0 copy-done.1
  99.6 12.7 %weight_grad.4.refs_0_ = bf16[3072,2048]{1,0:T(8,128)(2,1)S(1)} custom-call(bf16[640,3072]{1,0:T(8,128)(2,1)S(1)} %copy-done.1, bf16[640,2048]{1,0:T(8,128)(2,1)S(1)} %in_token_order.8.block), custom_call_target="tpu_custom_call" | custom-call | flops 1 | bytes 1 | tf_op jit(solution)/shard_map/weight_grad/pallas_call | solution.py:306
  112.3 0.0 collective-permute-done.9.refs_0_
  112.3 1.3 collective-permute-start.13
  113.6 0.9 collective-permute-start.11
  114.5 3.8 %collective-permute-done.7.refs_2_ = bf16[320,2048]{1,0:T(8,128)(2,1)S(1)} collective-permute-done((bf16[320,2048]{1,0:T(8,128)(2,1)S(1)}, bf16[320,2048]{1,0:T(8,128)(2,1)S(1)}, u32[]{:S(2)}, u32[]{:S(2)}) %collective-permute-start.7) | collective-permute-done | bytes 1310752 | tf_op jit(solution)/shard_map/ppermute | solution.py:371
  118.3 0.0 collective-permute-done.8.hidden
  118.3 0.0 slice-start
  118.3 0.3 in_token_order.9.block
  118.7 0.0 slice-start.1
  118.7 0.0 slice-start.2
  118.7 0.0 slice-start.3
  118.7 14.7 %weight_grad.6 = (bf16[3072,1024]{1,0:T(8,128)(2,1)}, bf16[3072,1024]{1,0:T(8,128)(2,1)S(1)}) custom-call(bf16[640,3072]{1,0:T(8,128)(2,1)} %collective-permute-done.8.hidden, bf16[640,2048]{1,0:T(8,128)(2,1)S(1)} %in_token_order.9.block, bf16[3072,2048]{1,0:T(8,128)(2,1)S(1)} %weight_grad.4.refs_0_), custom_call_target="tpu_custom_call" | custom-call | flops 1 | bytes 1 | tf_op jit(solution)/shard_map/weight_grad/pallas_call | solution.py:306
  133.4 0.0 collective-permute-start.10
  133.4 0.0 collective-permute-done.11.hidden
  133.4 2.5 %weight_grad.7 = (bf16[512,1024]{1,0:T(8,128)(2,1)}, bf16[512,1024]{1,0:T(8,128)(2,1)S(1)}) custom-call(bf16[640,512]{1,0:T(8,128)(2,1)S(1)} %collective-permute-done.11.hidden, bf16[640,2048]{1,0:T(8,128)(2,1)S(1)} %in_token_order.9.block, bf16[512,2048]{1,0:T(8,128)(2,1)S(1)} %weight_grad.5.refs_1_.refs_0_), custom_call_target="tpu_custom_call" | custom-call | flops 1 | bytes 1 | tf_op jit(solution)/shard_map/weight_grad/pallas_call | solution.py:306
  135.9 0.5 collective-permute-start.12
  136.4 9.0 %collective-permute-done.13.refs_1_ = bf16[320,2048]{1,0:T(8,128)(2,1)S(1)} collective-permute-done((bf16[320,2048]{1,0:T(8,128)(2,1)S(1)}, bf16[320,2048]{1,0:T(8,128)(2,1)S(1)}, u32[]{:S(2)}, u32[]{:S(2)}) %collective-permute-start.13) | collective-permute-done | bytes 1310752 | tf_op jit(solution)/shard_map/ppermute | solution.py:371
  145.4 0.0 slice-done
  145.4 0.0 slice-done.1
  145.4 0.0 slice-done.2
  145.4 0.0 slice-done.3
  145.4 0.0 copy-start.3
  145.4 1.2 copy-done.3
  146.6 11.3 %hidden_grad_late.1 = (bf16[640,3584]{1,0:T(8,128)(2,1)}, bf16[640,3584]{1,0:T(8,128)(2,1)}) custom-call(bf16[320,2048]{1,0:T(8,128)(2,1)S(1)} %collective-permute-done.9.refs_0_, bf16[320,2048]{1,0:T(8,128)(2,1)S(1)} %collective-permute-done.13.refs_1_, bf16[3584,2048]{1,0:T(8,128)(2,1)S(1)} %bitcast.9, ...), custom_call_target="tpu_custom_call", output_to_operand_aliasing={{0}: (7, {}), {1}: (8, {})} | custom-call | flops 999999995904 | bytes 1000000000 | tf_op jit(solution)/shard_map/hidden_grad_late/pallas_call | solution.py:257
  157.9 0.0 collective-permute-done.12.b_ref
  157.9 0.0 collective-permute-done.10.b_ref
  157.9 7.5 %add_rows.2.refs_0_ = bf16[3584,1024]{1,0:T(8,128)(2,1)} custom-call(bf16[3072,1024]{1,0:T(8,128)(2,1)S(1)} %get-tuple-element.101.a_ref, bf16[3072,1024]{1,0:T(8,128)(2,1)} %collective-permute-done.10.b_ref), custom_call_target="tpu_custom_call" | custom-call | flops 1 | bytes 1 | tf_op jit(solution)/shard_map/add_rows/pallas_call | solution.py:332
  165.4 2.5 %add_rows.3 = bf16[3584,1024]{1,0:T(8,128)(2,1)} custom-call(bf16[512,1024]{1,0:T(8,128)(2,1)S(1)} %get-tuple-element.99.a_ref, bf16[512,1024]{1,0:T(8,128)(2,1)} %collective-permute-done.12.b_ref, bf16[3584,1024]{1,0:T(8,128)(2,1)} %add_rows.2.refs_0_), custom_call_target="tpu_custom_call", output_to_operand_aliasing={{}: (2, {})} | custom-call | flops 1 | bytes 1 | tf_op jit(solution)/shard_map/add_rows/pallas_call | solution.py:332
  (3 shorter events, 0.0 us)
Async XLA Ops:
  2.9 18.0 %collective-permute-start = (bf16[160,2048]{1,0:T(8,128)(2,1)}, bf16[160,2048]{1,0:T(8,128)(2,1)}, u32[]{:S(2)}, u32[]{:S(2)}) collective-permute-start(bf16[160,2048]{1,0:T(8,128)(2,1)} %get-tuple-element.64.refs_0_), channel_id=1, source_target_pairs={{0,2},{1,3},{2,0},{3,1},{4,6},{5,7},{6,4},{7,5},{8,10},{9,11},{10,... | collective-permute-start | bytes 1966088 | tf_op jit(solution)/shard_map/ppermute | solution.py:356
  5.9 16.9 %collective-permute-start.2 = (bf16[160,2048]{1,0:T(8,128)(2,1)S(1)}, bf16[160,2048]{1,0:T(8,128)(2,1)S(1)}, u32[]{:S(2)}, u32[]{:S(2)}) collective-permute-start(bf16[160,2048]{1,0:T(8,128)(2,1)S(1)} %get-tuple-element.56.refs_0_), channel_id=1, source_target_pairs={{0,4},{4,0},{8,12},{12,8},{1,5},{5,1},{9,13},{13,9},{2,6},{6,2},{1... | collective-permute-start | bytes 1966088 | tf_op jit(solution)/shard_map/ppermute | solution.py:369
  20.9 18.0 %collective-permute-start.1 = (bf16[160,2048]{1,0:T(8,128)(2,1)}, bf16[160,2048]{1,0:T(8,128)(2,1)}, u32[]{:S(2)}, u32[]{:S(2)}) collective-permute-start(bf16[160,2048]{1,0:T(8,128)(2,1)} %collective-permute-done.refs_0_), channel_id=1, source_target_pairs={{0,4},{4,0},{8,12},{12,8},{1,5},{5,1},{9,13},{13,9},{2,6},{6,2},{1... | collective-permute-start | bytes 1966088 | tf_op jit(solution)/shard_map/ppermute | solution.py:369
  22.7 28.4 %collective-permute-start.5 = (bf16[160,2048]{1,0:T(8,128)(2,1)}, bf16[160,2048]{1,0:T(8,128)(2,1)}, u32[]{:S(2)}, u32[]{:S(2)}) collective-permute-start(bf16[160,2048]{1,0:T(8,128)(2,1)} %get-tuple-element.64.refs_0_), channel_id=1, source_target_pairs={{0,4},{4,0},{8,12},{12,8},{1,5},{5,1},{9,13},{13,9},{2,6},{6,2},{1... | collective-permute-start | bytes 1966088 | tf_op jit(solution)/shard_map/ppermute | solution.py:369
  25.3 25.9 %collective-permute-start.4 = (bf16[320,2048]{1,0:T(8,128)(2,1)}, bf16[320,2048]{1,0:T(8,128)(2,1)}, u32[]{:S(2)}, u32[]{:S(2)}) collective-permute-start(bf16[320,2048]{1,0:T(8,128)(2,1)} %in_token_order.6.refs_0_), channel_id=1, source_target_pairs={{4,8},{8,4},{5,9},{9,5},{6,10},{10,6},{7,11},{11,7},{20,24},{24,20... | collective-permute-start | bytes 3932168 | tf_op jit(solution)/shard_map/ppermute | solution.py:370
  27.0 91.3 %collective-permute-start.8 = (bf16[640,3072]{1,0:T(8,128)(2,1)}, bf16[640,3072]{1,0:T(8,128)(2,1)}, u32[]{:S(2)}, u32[]{:S(2)}) collective-permute-start(bf16[640,3072]{1,0:T(8,128)(2,1)} %get-tuple-element.78.hidden), channel_id=1, source_target_pairs={{0,2},{1,3},{2,0},{3,1},{4,6},{5,7},{6,4},{7,5},{8,10},{9,11},{10,... | collective-permute-start | bytes 11796488 | tf_op jit(solution)/shard_map/ppermute | solution.py:356
  37.4 31.5 %copy-start = (bf16[3584,2048]{1,0:T(8,128)(2,1)}, bf16[3584,2048]{1,0:T(8,128)(2,1)S(1)}, u32[]{:S(2)}) copy-start(bf16[3584,2048]{1,0:T(8,128)(2,1)S(1)} %get-tuple-element.68.refs_3_.refs_2_) | copy-start | bytes 44040196
  41.3 27.6 %collective-permute-start.3 = (bf16[320,2048]{1,0:T(8,128)(2,1)S(1)}, bf16[320,2048]{1,0:T(8,128)(2,1)S(1)}, u32[]{:S(2)}, u32[]{:S(2)}) collective-permute-start(bf16[320,2048]{1,0:T(8,128)(2,1)S(1)} %in_token_order.5.refs_0_), channel_id=1, source_target_pairs={{4,8},{8,4},{5,9},{9,5},{6,10},{10,6},{7,11},{11,7},{20,24},{24,20... | collective-permute-start | bytes 3932168 | tf_op jit(solution)/shard_map/ppermute | solution.py:370
  51.2 35.1 %collective-permute-start.6 = (bf16[320,2048]{1,0:T(8,128)(2,1)}, bf16[320,2048]{1,0:T(8,128)(2,1)S(1)}, u32[]{:S(2)}, u32[]{:S(2)}) collective-permute-start(bf16[320,2048]{1,0:T(8,128)(2,1)} %collective-permute-done.4.refs_0_.refs_1_), channel_id=1, source_target_pairs={{4,0},{8,12},{5,1},{9,13},{6,2},{10,14},{7,3},{11,15},{20,16},{24,... | collective-permute-start | bytes 3932168 | tf_op jit(solution)/shard_map/ppermute | solution.py:371
  86.3 26.0 %collective-permute-start.9 = (bf16[320,2048]{1,0:T(8,128)(2,1)S(1)}, bf16[320,2048]{1,0:T(8,128)(2,1)S(1)}, u32[]{:S(2)}, u32[]{:S(2)}) collective-permute-start(bf16[320,2048]{1,0:T(8,128)(2,1)S(1)} %in_token_order.7.refs_1_), channel_id=1, source_target_pairs={{4,8},{8,4},{5,9},{9,5},{6,10},{10,6},{7,11},{11,7},{20,24},{24,20... | collective-permute-start | bytes 3932168 | tf_op jit(solution)/shard_map/ppermute | solution.py:370
  87.0 31.3 %collective-permute-start.7 = (bf16[320,2048]{1,0:T(8,128)(2,1)S(1)}, bf16[320,2048]{1,0:T(8,128)(2,1)S(1)}, u32[]{:S(2)}, u32[]{:S(2)}) collective-permute-start(bf16[320,2048]{1,0:T(8,128)(2,1)S(1)} %collective-permute-done.3.refs_1_), channel_id=1, source_target_pairs={{4,0},{8,12},{5,1},{9,13},{6,2},{10,14},{7,3},{11,15},{20,16},{24,... | collective-permute-start | bytes 3932168 | tf_op jit(solution)/shard_map/ppermute | solution.py:371
  95.9 1.6 copy-start.2
  95.9 3.7 %copy-start.1 = (bf16[640,3072]{1,0:T(8,128)(2,1)S(1)}, bf16[640,3072]{1,0:T(8,128)(2,1)}, u32[]{:S(2)}) copy-start(bf16[640,3072]{1,0:T(8,128)(2,1)} %get-tuple-element.78.hidden) | copy-start | bytes 11796484
  112.3 33.0 %collective-permute-start.13 = (bf16[320,2048]{1,0:T(8,128)(2,1)S(1)}, bf16[320,2048]{1,0:T(8,128)(2,1)S(1)}, u32[]{:S(2)}, u32[]{:S(2)}) collective-permute-start(bf16[320,2048]{1,0:T(8,128)(2,1)S(1)} %collective-permute-done.9.refs_0_), channel_id=1, source_target_pairs={{4,0},{8,12},{5,1},{9,13},{6,2},{10,14},{7,3},{11,15},{20,16},{24,... | collective-permute-start | bytes 3932168 | tf_op jit(solution)/shard_map/ppermute | solution.py:371
  113.6 19.8 %collective-permute-start.11 = (bf16[640,512]{1,0:T(8,128)(2,1)S(1)}, bf16[640,512]{1,0:T(8,128)(2,1)S(1)}, u32[]{:S(2)}, u32[]{:S(2)}) collective-permute-start(bf16[640,512]{1,0:T(8,128)(2,1)S(1)} %copy-done.2), channel_id=1, source_target_pairs={{0,2},{1,3},{2,0},{3,1},{4,6},{5,7},{6,4},{7,5},{8,10},{9,11},{10,... | collective-permute-start | bytes 1966088 | tf_op jit(solution)/shard_map/ppermute | solution.py:356
  118.3 27.1 %slice-start = ((s8[14680064]{0:T(1024)(128)(4,1)}), s8[4194304]{0:T(1024)(128)(4,1)S(1)}, s32[]{:S(2)}) async-start(s8[14680064]{0:T(1024)(128)(4,1)} %bitcast.8), calls=%async_computation | async-start | bytes 8388608
  118.7 26.7 %slice-start.1 = ((s8[14680064]{0:T(1024)(128)(4,1)}), s8[4194304]{0:T(1024)(128)(4,1)S(1)}, s32[]{:S(2)}) async-start(s8[14680064]{0:T(1024)(128)(4,1)} %bitcast.8), calls=%async_computation.1 | async-start | bytes 8388608
  118.7 26.7 %slice-start.2 = ((s8[14680064]{0:T(1024)(128)(4,1)}), s8[4194304]{0:T(1024)(128)(4,1)S(1)}, s32[]{:S(2)}) async-start(s8[14680064]{0:T(1024)(128)(4,1)} %bitcast.8), calls=%async_computation.2 | async-start | bytes 8388608
  118.7 26.7 %slice-start.3 = ((s8[14680064]{0:T(1024)(128)(4,1)}), s8[2097152]{0:T(1024)(128)(4,1)S(1)}, s32[]{:S(2)}) async-start(s8[14680064]{0:T(1024)(128)(4,1)} %bitcast.8), calls=%async_computation.3 | async-start | bytes 4194304
  133.4 24.5 %collective-permute-start.10 = (bf16[3072,1024]{1,0:T(8,128)(2,1)}, bf16[3072,1024]{1,0:T(8,128)(2,1)}, u32[]{:S(2)}, u32[]{:S(2)}) collective-permute-start(bf16[3072,1024]{1,0:T(8,128)(2,1)} %get-tuple-element.85), channel_id=1, source_target_pairs={{0,1},{1,0},{2,3},{3,2},{4,5},{5,4},{6,7},{7,6},{8,9},{9,8},{10,11... | collective-permute-start | bytes 18874376 | tf_op jit(solution)/shard_map/ppermute | solution.py:361
  135.9 22.0 %collective-permute-start.12 = (bf16[512,1024]{1,0:T(8,128)(2,1)}, bf16[512,1024]{1,0:T(8,128)(2,1)}, u32[]{:S(2)}, u32[]{:S(2)}) collective-permute-start(bf16[512,1024]{1,0:T(8,128)(2,1)} %get-tuple-element.92.refs_6_), channel_id=1, source_target_pairs={{0,1},{1,0},{2,3},{3,2},{4,5},{5,4},{6,7},{7,6},{8,9},{9,8},{10,11... | collective-permute-start | bytes 3145736 | tf_op jit(solution)/shard_map/ppermute | solution.py:361
  145.4 1.2 copy-start.3

commit v3 on v2

--- a/solution.py
+++ b/solution.py
@@ -11,6 +11,7 @@
 VMEM_LIMIT = 10 * 1024 * 1024
 F32, BF16 = jnp.float32, jnp.bfloat16
 SHORT = pl.CostEstimate(flops=1, bytes_accessed=1, transcendentals=0)
+BRIEF = pl.CostEstimate(flops=1, bytes_accessed=10**6, transcendentals=0)
 LONG = pl.CostEstimate(flops=10**12, bytes_accessed=10**9, transcendentals=0)
 ANY_SPEC = pl.BlockSpec(memory_space=pl.ANY)
 VMEM_SPEC = pl.BlockSpec(memory_space=pltpu.VMEM)
@@ -44,7 +45,7 @@
     return [pltpu.with_memory_space_constraint(v, pltpu.HBM) for v in values]
 
 
-def place_shards(parts, half, into, sem, start, by_core=False):
+def place_shards(parts, half, into, sem, start, by_core=False, swapped_from=0):
     act = (lambda c: c.start()) if start else (lambda c: c.wait())
     z = lax.axis_index("tensor")
     pair = z // 2
@@ -71,44 +72,97 @@
         if whole:
             rows = parts[0].shape[0]
             place(parts.pop(0), base + (z % 2) * rows)
-            place(parts.pop(0), base + (1 - z % 2) * rows)
+            place(parts.pop(0).at[pl.ds(swapped_from, rows)], base + (1 - z % 2) * rows)
         else:
             place(parts.pop(0), base)
     if half != "early":
         base = 0 if half == "late" else (1 - pair) * (into.shape[0] // 2)
         middle = jnp.logical_or(z == 1, z == 2)
-        rows = parts[0].shape[0]
-        steps = [base] if len(parts) == 2 else [base + pair * rows, base + (1 - pair) * rows]
-        n = len(parts) // 2
+        if len(parts) == 3:
+            place(parts[2], base + parts[0].shape[0])
 
         @pl.when(middle)
         def _():
-            for ref, row in zip(parts[:n], steps):
-                place(ref, row)
+            place(parts[0], base)
 
         @pl.when(jnp.logical_not(middle))
         def _():
-            for ref, row in zip(parts[n:], steps):
-                place(ref, row)
-
-
-def move_kernel(half, by_core, n_parts, *refs):
+            place(parts[1], base)
+
+
+def move_kernel(half, by_core, swapped_from, n_parts, *refs):
     parts, (into, sem) = refs[:n_parts], refs[-2:]
     for start in (True, False):
-        place_shards(parts, half, into, sem, start, by_core)
-
-
-def in_token_order(half, rows, parts, by_core=False, wait_for=()):
+        place_shards(parts, half, into, sem, start, by_core, swapped_from)
+
+
+def in_token_order(half, rows, parts, by_core=False, swapped_from=0, wait_for=(), cost=None):
     cols = parts[0].shape[1]
     return pl.pallas_call(
-        functools.partial(move_kernel, half, by_core, len(parts)),
+        functools.partial(move_kernel, half, by_core, swapped_from, len(parts)),
         in_specs=[ANY_SPEC] * (len(parts) + len(wait_for)),
         out_specs=VMEM_SPEC,
         out_shape=pltpu.VMEM((rows, cols), BF16),
         scratch_shapes=[pltpu.SemaphoreType.DMA((16,))],
+        cost_estimate=cost,
         compiler_params=pltpu.CompilerParams(vmem_limit_bytes=VMEM_LIMIT),
         name="in_token_order",
-    )(*parts, *wait_for)
+    )(*parts, *in_hbm(wait_for))
+
+
+def stack_kernel(*refs):
+    parts, into, sem = refs[:-2], refs[-2], refs[-1]
+    copies = []
+    for k, part in enumerate(parts):
+        rows = part.shape[0]
+        copies.append(pltpu.make_async_copy(part, into.at[pl.ds(k * rows, rows)], sem.at[k]))
+    for copy in copies:
+        copy.start()
+    for copy in copies:
+        copy.wait()
+
+
+def stack(parts):
+    rows, cols = parts[0].shape
+    return pl.pallas_call(
+        stack_kernel,
+        in_specs=[ANY_SPEC] * len(parts),
+        out_specs=VMEM_SPEC,
+        out_shape=pltpu.VMEM((rows * len(parts), cols), BF16),
+        scratch_shapes=[pltpu.SemaphoreType.DMA((len(parts),))],
+        compiler_params=pltpu.CompilerParams(vmem_limit_bytes=VMEM_LIMIT),
+        name="stack",
+    )(*parts)
+
+
+def take_rows_kernel(row, *refs):
+    parts, out, sem = refs[:-2], refs[-2], refs[-1]
+    z = lax.axis_index("tensor")
+    middle = jnp.logical_or(z == 1, z == 2)
+    here = [None] if len(parts) == 1 else [middle, jnp.logical_not(middle)]
+
+    def take(part):
+        copy = pltpu.make_async_copy(part.at[pl.ds(row, out.shape[0])], out, sem)
+        copy.start()
+        copy.wait()
+
+    for part, condition in zip(parts, here):
+        if condition is None:
+            take(part)
+        else:
+            pl.when(condition)(functools.partial(take, part))
+
+
+def take_rows(parts, row, rows):
+    return pl.pallas_call(
+        functools.partial(take_rows_kernel, row),
+        in_specs=[ANY_SPEC] * len(parts),
+        out_specs=VMEM_SPEC,
+        out_shape=pltpu.VMEM((rows, parts[0].shape[1]), BF16),
+        scratch_shapes=[pltpu.SemaphoreType.DMA],
+        compiler_params=pltpu.CompilerParams(vmem_limit_bytes=VMEM_LIMIT),
+        name="take_rows",
+    )(*parts)
 
 
 def mark_kernel(*refs):
@@ -120,8 +174,8 @@
     return pl.pallas_call(
         mark_kernel,
         in_specs=[ANY_SPEC] * len(values),
-        out_specs=VMEM_SPEC,
-        out_shape=jax.ShapeDtypeStruct((8, 128), F32),
+        out_specs=pl.BlockSpec((8, 128), lambda: (0, 0)),
+        out_shape=pltpu.HBM((8, 128), F32),
         cost_estimate=pl.CostEstimate(flops=1, bytes_accessed=cost, transcendentals=0),
         compiler_params=pltpu.CompilerParams(vmem_limit_bytes=VMEM_LIMIT),
         name="mark",
@@ -148,34 +202,30 @@
     return pl.pallas_call(
         load_weight_kernel,
         in_specs=[ANY_SPEC],
-        out_specs=[VMEM_SPEC] * (blocks + 1),
-        out_shape=[pltpu.VMEM((ff, d // blocks), BF16)] * blocks + [jax.ShapeDtypeStruct((8, 128), F32)],
+        out_specs=[VMEM_SPEC] * blocks + [pl.BlockSpec((8, 128), lambda: (0, 0))],
+        out_shape=[pltpu.VMEM((ff, d // blocks), BF16)] * blocks + [pltpu.HBM((8, 128), F32)],
         scratch_shapes=[pltpu.SemaphoreType.DMA((blocks,))],
-        cost_estimate=LONG,
+        cost_estimate=SHORT,
         compiler_params=pltpu.CompilerParams(vmem_limit_bytes=VMEM_LIMIT),
         name="load_weight",
     )(*in_hbm([weight]))
 
 
-def hidden_kernel(gate_ref, up_ref, *hidden_refs):
-    at = 0
-    for ref in hidden_refs:
-        columns = slice(at, at + ref.shape[1])
-        gate, up = gate_ref[:, columns].astype(F32), up_ref[:, columns].astype(F32)
-        ref[...] = (gate * sigmoid(gate) * up).astype(BF16)
-        at += ref.shape[1]
-
-
-def hidden_chunks(gate, up, widths):
+def hidden_kernel(gate_ref, up_ref, hidden_ref):
+    gate, up = gate_ref[...].astype(F32), up_ref[...].astype(F32)
+    hidden_ref[...] = (gate * sigmoid(gate) * up).astype(BF16)
+
+
+def hidden_of(gate, up):
     tok, ff = gate.shape
     rows = next(r for r in (64, 32, 16) if tok % r == 0)
-    spec = lambda w: pl.BlockSpec((rows, w), lambda i: (i, 0))
+    spec = pl.BlockSpec((rows, ff), lambda i: (i, 0))
     return pl.pallas_call(
         hidden_kernel,
         grid=(tok // rows,),
-        in_specs=[spec(ff)] * 2,
-        out_specs=[spec(w) for w in widths],
-        out_shape=[pltpu.HBM((tok, w), BF16) for w in widths],
+        in_specs=[spec] * 2,
+        out_specs=spec,
+        out_shape=pltpu.HBM((tok, ff), BF16),
         cost_estimate=SHORT,
         compiler_params=pltpu.CompilerParams(vmem_limit_bytes=VMEM_LIMIT),
         name="hidden",
@@ -245,7 +295,7 @@
         in_specs += [block] * 2
         args += in_hbm(by)
     in_specs += [ANY_SPEC] * len(wait_for)
-    args += wait_for
+    args += in_hbm(wait_for)
     if by is not None:
         out_shape, out_specs = [pltpu.HBM((tok, ff), BF16)] * 2, [block] * 2
         if outs is not None:
@@ -300,7 +350,7 @@
         args.append(in_vmem(start))
     if split:
         out_specs = [pl.BlockSpec((tile, cols // 2), lambda i: (i, 0))] * 2
-        out_shape = [pltpu.HBM((ff, cols // 2), BF16), jax.ShapeDtypeStruct((ff, cols // 2), BF16)]
+        out_shape = [pltpu.HBM((ff, cols // 2), BF16), pltpu.VMEM((ff, cols // 2), BF16)]
     else:
         out_specs, out_shape = VMEM_SPEC, pltpu.VMEM((ff, cols), BF16)
     return pl.pallas_call(
@@ -315,31 +365,23 @@
     )(*args)
 
 
-def add_kernel(scale, a_ref, b_ref, *refs):
-    refs[-1][...] = ((a_ref[...].astype(F32) + b_ref[...].astype(F32)) * scale).astype(BF16)
-
-
-def add_rows(keep, got, scale, row, total_rows, out=None):
+def add_kernel(scale, a_ref, b_ref, out_ref):
+    out_ref[...] = ((a_ref[...].astype(F32) + b_ref[...].astype(F32)) * scale).astype(BF16)
+
+
+def scaled_sum(keep, got, scale):
     rows, cols = keep.shape
-    tile = pick_tile(math.gcd(rows, row), 512)
-    first = row // tile
-    spec = pl.BlockSpec((tile, cols), lambda i: (i, 0))
-    in_specs, args, aliases = [spec] * 2, [keep, got], {}
-    if out is not None:
-        aliases = {2: 0}
-        in_specs.append(ANY_SPEC)
-        args += in_hbm([out])
+    spec = pl.BlockSpec((pick_tile(rows, 896), cols), lambda i: (i, 0))
     return pl.pallas_call(
         functools.partial(add_kernel, scale),
-        grid=(rows // tile,),
-        in_specs=in_specs,
-        out_specs=pl.BlockSpec((tile, cols), lambda i: (i + first, 0)),
-        out_shape=pltpu.HBM((total_rows, cols), BF16),
-        input_output_aliases=aliases,
+        grid=(rows // spec.block_shape[0],),
+        in_specs=[spec] * 2,
+        out_specs=spec,
+        out_shape=pltpu.HBM((rows, cols), BF16),
         cost_estimate=SHORT,
-        compiler_params=pltpu.CompilerParams(vmem_limit_bytes=VMEM_LIMIT),
-        name="add_rows",
-    )(*args)
+        compiler_params=pltpu.CompilerParams(vmem_limit_bytes=VMEM_LIMIT * 3 // 2),
+        name="scaled_sum",
+    )(keep, got)
 
 
 def on_device(out_grad, gate_pre, up_pre, down_weight):
@@ -363,8 +405,8 @@
     def columns_of(which):
         return lax.dynamic_slice(grad, (0, which * cols), (grad.shape[0], cols))
 
-    if nt == 4 and chips == 2 and ff % 896 == 0:
-        cut = 6 * ff // 7
+    hidden = hidden_of(gate, up)
+    if nt == 4 and chips == 2:
         both_ways = lambda *pairs: [q for a, b in pairs for q in ((a, b), (b, a))]
         swap_pair = lambda v: lax.ppermute(v, "tensor", both_ways((0, 1), (2, 3)))
         swap_middle = lambda v: lax.ppermute(v, "tensor", both_ways((1, 2)))
@@ -372,51 +414,46 @@
 
         mine, rest = together(columns_of(chip), columns_of(1 - chip))
         far, a1 = shift(rest, 1), swap_pair(mine)
-        h0, h1 = hidden_chunks(gate, up, [cut, ff - cut])
-        far, h0 = together(far, h0)
-        a1, rest, first, weight, h1 = together(a1, rest, mark_of([far], 10**6), down_weight, h1)
-
-        h0_in = shift(h0, 1)
-        a3, a2 = swap_pair(far), swap_pair(rest)
+        both = stack([far, rest])
+        a1, first, weight = together(a1, mark_of([far], 10**6), down_weight)
+
+        hidden_in = shift(hidden, 1)
+        a23 = swap_pair(both)
         pair1 = in_token_order("early", tok // 2, [mine, a1], wait_for=[first])
         b1 = swap_middle(pair1)
         *weights, mark = load_weight(weight, chips)
-        a3, mark = together(a3, mark)
-
-        pair3 = in_token_order("early", tok // 2, [far, a3], wait_for=[mark])
+        a23, mark = together(a23, mark)
+
+        pair3 = in_token_order("early", tok // 2, [far, a23], wait_for=[mark])
         b3 = swap_middle(pair3)
-        b1, a2 = together(b1, a2)
+        pair2 = in_token_order("early", tok // 2, [rest, a23], swapped_from=tok // 4, cost=BRIEF)
+        b1, mark = together(b1, mark_of([pair2], 1))
 
         c1 = to_ends(b1)
-        pair2 = in_token_order("early", tok // 2, [rest, a2])
-        outs = hidden_grad("early", [[pair1], [pair2]], weights, tok, None, (gate, up))
-        b3, c1, outs, pair2, h1 = together(b3, c1, outs, pair2, h1)
-
-        c3, b2 = to_ends(b3), swap_middle(pair2)
-        h1_in = shift(h1, 1)
+        outs = hidden_grad("early", [[pair1], [pair2]], weights, tok, None, (gate, up), wait_for=[mark])
+        b3, c1, outs, pair2 = together(b3, c1, outs, pair2)
+
+        shard = tok // 4
+        c3, b2 = to_ends(b3), swap_middle(take_rows([pair2], 0, shard))
         partial = hidden_grad("late", [[b1, c1]], weights[:1], tok)
-        h0, h1, partial = together(h0, h1, partial)
+        hidden, partial = together(hidden, partial)
         block = in_token_order("all", tok, [pair1, b1, c1], by_core=True)
-        own0, own1 = weight_grad(block, h0, split=False), weight_grad(block, h1, split=False)
-        first = mark_of([own0, own1], 1)
+        own = weight_grad(block, hidden, split=False)
+        first = mark_of([own], 1)
         b2, partial, first = together(b2, partial, first)
 
         c2 = to_ends(b2)
-        c3, h0_in, partial, first = together(c3, h0_in, partial, first)
+        c3, hidden_in, partial, first = together(c3, hidden_in, partial, first)
+        rest2 = shift(take_rows([b3, c3], shard, shard), 1)
         block = in_token_order("all", tok, [pair3, b3, c3], by_core=True, wait_for=[first])
-        send0, keep0 = weight_grad(block, h0_in, own0)
-        got0 = swap_cores(send0)
-        send0, h1_in = together(send0, h1_in)
-        send1, keep1 = weight_grad(block, h1_in, own1)
-        got1 = swap_cores(send1)
-        c2, send1, partial = together(c2, send1, partial)
-        outs = hidden_grad("late", [[b2, c2]], weights[1:], tok, partial, (gate, up), outs, [send1])
-        got0, got1, outs = together(got0, got1, outs)
-        down_grad = add_rows(keep0, got0, scale, 0, ff)
-        down_grad = add_rows(keep1, got1, scale, cut, ff, down_grad)
+        send, keep = weight_grad(block, hidden_in, own)
+        got = swap_cores(send)
+        c2, rest2, send, partial = together(c2, rest2, send, partial)
+        outs = hidden_grad("late", [[b2, c2, rest2]], weights[1:], tok, partial, (gate, up), outs, [send])
+        got, outs = together(got, outs)
+        down_grad = scaled_sum(keep, got, scale)
     else:
         gather = lambda v: lax.all_gather(v, "tensor", axis=0, tiled=True)
-        (hidden,) = hidden_chunks(gate, up, [ff])
         hiddens = [hidden] + [shift(hidden, s) for s in range(1, chips)]
 
         def by_core(value):
@@ -429,7 +466,7 @@
             total = weight_grad(block, part, total, split=False)
         send, keep = weight_grad(blocks[-1], hiddens[-1], total)
         outs = hidden_grad("all", [[gather(grad)]], load_weight(down_weight, 1)[:1], tok, None, (gate, up))
-        down_grad = add_rows(keep, swap_cores(send), scale, 0, ff)
+        down_grad = scaled_sum(keep, swap_cores(send), scale)
     return (outs[0][None], outs[1][None], down_grad)
 
 

time: 169 us -> 158 us (0.935)
  Pallas kernels: 102 us -> 95 us
  waiting for transfers between devices: 44.9 us -> 42.1 us
    ppermute x3, waiting for transfers between devices: 30.1 us -> 18.5 us  [on_device(): to_ends = lambda v: lax.ppermute(v, 'tensor', [(1, 0), (2, 3)])]
    pallas_call x8 -> x10, Pallas kernels: 26.7 us -> 20 us  [the longest x1 9.49 us: hidden_of(): pl.pallas_call(hidden_kernel, grid=(tok // rows,), in_specs=[spec] * 2, o...]
    ppermute x3 -> x2, waiting for transfers between devices: 10.6 us -> 15.1 us  [on_device(): swap_pair = lambda v: lax.ppermute(v, 'tensor', both_ways((0, 1), (2, 3)))]
    ppermute x3, waiting for transfers between devices: 4.17 us -> 8.32 us  [shift(): lax.ppermute(value, 'dp', [(2 * c + k, 2 * ((c + s) % chips) + k) for c i...]
    pallas_call x4 -> x2, Pallas kernels: 32 us -> 29.5 us  [weight_grad(): pl.pallas_call(functools.partial(weight_grad_kernel, tile, start is not N...]
    pallas_call x2 -> x3, Pallas kernels: 0.01 us -> 1.78 us  [mark_of(): pl.pallas_call(mark_kernel, in_specs=[ANY_SPEC] * len(values), out_specs=...]
    ppermute x3 -> x2, starting transfers between devices: 4.29 us -> 3.79 us  [on_device(): swap_pair = lambda v: lax.ppermute(v, 'tensor', both_ways((0, 1), (2, 3)))]
  transfers between devices with their start and end apart: 14 -> 12, of which waited for: 6 -> 6; matrix products, arithmetic and copies ran while one was open for 0% -> 0% of each run, Pallas kernels for 55% -> 56%
where the time goes in v3:
time: 158 us; the launch traced here: 157 us
  Pallas kernels  95 us (60%)
  waiting for transfers between devices  42.1 us (27%)
  starting transfers between devices  15.3 us (10%)
  local copies, waits for them, and re-layouts  3.72 us (2%)
    pallas_call x3, Pallas kernels, hidden_grad(): pl.pallas_call(functools.partial(hidden_grad_kernel, half, tuple((len(s)...  33.8 us
    pallas_call x2, Pallas kernels, weight_grad(): pl.pallas_call(functools.partial(weight_grad_kernel, tile, start is not N...  29.5 us
    ppermute x3, waiting for transfers between devices, on_device(): to_ends = lambda v: lax.ppermute(v, 'tensor', [(1, 0), (2, 3)])  18.5 us
    ppermute x2, waiting for transfers between devices, on_device(): swap_pair = lambda v: lax.ppermute(v, 'tensor', both_ways((0, 1), (2, 3)))  15.1 us
    pallas_call x1, Pallas kernels, load_weight(): pl.pallas_call(load_weight_kernel, in_specs=[ANY_SPEC], out_specs=[VMEM_S...  9.98 us
    pallas_call x1, Pallas kernels, hidden_of(): pl.pallas_call(hidden_kernel, grid=(tok // rows,), in_specs=[spec] * 2, o...  9.49 us
    ppermute x3, waiting for transfers between devices, shift(): lax.ppermute(value, 'dp', [(2 * c + k, 2 * ((c + s) % chips) + k) for c i...  8.32 us
    pallas_call x1, Pallas kernels, scaled_sum(): pl.pallas_call(functools.partial(add_kernel, scale), grid=(rows // spec.b...  7.24 us
  transfers between devices with their start and end apart: 12, of which 6 were waited for; matrix products, arithmetic and copies ran while one was open for 0% of the time, Pallas kernels for 56%

profile of v3, /device:TPU:0, one launch (start us, length us, event | category | flops | bytes accessed | tf_op | source)
XLA Modules:
  0.0 157.0 jit_solution(15165966895288902215)
XLA Ops:
  0.7 1.4 dynamic-slice_bitcast_fusion
  2.1 3.0 %collective-permute-start = (bf16[160,2048]{1,0:T(8,128)(2,1)S(1)}, bf16[160,2048]{1,0:T(8,128)(2,1)S(1)}, u32[]{:S(2)}, u32[]{:S(2)}) collective-permute-start(bf16[160,2048]{1,0:T(8,128)(2,1)S(1)} %get-tuple-element.42.refs_1_.refs_0_), channel_id=1, source_target_pairs={{0,2},{1,3},{2,0},{3,1},{4,6},{5,7},{6,4},{7,5},{8,10},{9,11},{10,... | collective-permute-start | bytes 1966088 | tf_op jit(solution)/shard_map/ppermute | solution.py:398
  5.1 1.6 %collective-permute-start.2 = (bf16[160,2048]{1,0:T(8,128)(2,1)S(1)}, bf16[160,2048]{1,0:T(8,128)(2,1)S(1)}, u32[]{:S(2)}, u32[]{:S(2)}) collective-permute-start(bf16[160,2048]{1,0:T(8,128)(2,1)S(1)} %get-tuple-element.43.refs_0_), channel_id=1, source_target_pairs={{0,4},{4,0},{8,12},{12,8},{1,5},{5,1},{9,13},{13,9},{2,6},{6,2},{1... | collective-permute-start | bytes 1966088 | tf_op jit(solution)/shard_map/ppermute | solution.py:411
  6.7 9.5 %hidden.1 = bf16[640,3584]{1,0:T(8,128)(2,1)} custom-call(bf16[640,3584]{1,0:T(8,128)(2,1)} %bitcast.10, bf16[640,3584]{1,0:T(8,128)(2,1)} %bitcast.13), custom_call_target="tpu_custom_call" | custom-call | flops 1 | bytes 1 | tf_op jit(solution)/shard_map/hidden/pallas_call | solution.py:223
  16.2 0.5 collective-permute-start.7
  16.7 4.0 %collective-permute-done.refs_0_ = bf16[160,2048]{1,0:T(8,128)(2,1)S(1)} collective-permute-done((bf16[160,2048]{1,0:T(8,128)(2,1)S(1)}, bf16[160,2048]{1,0:T(8,128)(2,1)S(1)}, u32[]{:S(2)}, u32[]{:S(2)}) %collective-permute-start) | collective-permute-done | bytes 655392 | tf_op jit(solution)/shard_map/ppermute | solution.py:398
  20.6 0.4 stack.1
  21.1 2.2 %collective-permute-start.1 = (bf16[320,2048]{1,0:T(8,128)(2,1)S(1)}, bf16[320,2048]{1,0:T(8,128)(2,1)S(1)}, u32[]{:S(2)}, u32[]{:S(2)}) collective-permute-start(bf16[320,2048]{1,0:T(8,128)(2,1)S(1)} %stack.1), channel_id=1, source_target_pairs={{0,4},{4,0},{8,12},{12,8},{1,5},{5,1},{9,13},{13,9},{2,6},{6,2},{1... | collective-permute-start | bytes 3932168 | tf_op jit(solution)/shard_map/ppermute | solution.py:411
  23.3 0.6 mark.3.refs_2_
  23.9 0.0 collective-permute-done.2.refs_1_
  23.9 0.6 in_token_order.6.refs_0_
  24.4 0.7 collective-permute-start.4
  25.2 10.0 %load_weight.1 = (bf16[3584,2048]{1,0:T(8,128)(2,1)S(1)}, bf16[3584,2048]{1,0:T(8,128)(2,1)S(1)}, f32[8,128]{1,0:T(8,128)}) custom-call(bf16[3584,4096]{1,0:T(8,128)(2,1)} %weight), custom_call_target="tpu_custom_call" | custom-call | flops 1 | bytes 1 | tf_op jit(solution)/shard_map/load_weight/pallas_call | solution.py:202
  35.2 15.1 %collective-permute-done.1.refs_1_ = bf16[320,2048]{1,0:T(8,128)(2,1)S(1)} collective-permute-done((bf16[320,2048]{1,0:T(8,128)(2,1)S(1)}, bf16[320,2048]{1,0:T(8,128)(2,1)S(1)}, u32[]{:S(2)}, u32[]{:S(2)}) %collective-permute-start.1) | collective-permute-done | bytes 1310752 | tf_op jit(solution)/shard_map/ppermute | solution.py:411
  50.3 0.6 in_token_order.7.refs_0_.refs_1_
  50.8 0.6 mark.4.refs_6_
  51.4 0.0 collective-permute-done.4.refs_0_.refs_1_
  51.4 1.3 collective-permute-start.5
  52.7 0.6 in_token_order.5.refs_0_
  53.3 0.7 collective-permute-start.3
  54.1 14.5 %hidden_grad_early.1 = (bf16[640,3584]{1,0:T(8,128)(2,1)}, bf16[640,3584]{1,0:T(8,128)(2,1)}) custom-call(bf16[320,2048]{1,0:T(8,128)(2,1)S(1)} %in_token_order.6.refs_0_, bf16[320,2048]{1,0:T(8,128)(2,1)S(1)} %in_token_order.7.refs_0_.refs_1_, bf16[3584,2048]{1,0:T(8,128)(2,1)S(1)} %get-tuple-element.51.refs_2_, ...), custom_call_target="tpu_custom_call" | custom-call | flops 1 | bytes 1 | tf_op jit(solution)/shard_map/hidden_grad_early/pallas_call | solution.py:307
  68.6 14.5 %collective-permute-done.5.refs_1_.refs_2_ = bf16[320,2048]{1,0:T(8,128)(2,1)S(1)} collective-permute-done((bf16[320,2048]{1,0:T(8,128)(2,1)S(1)}, bf16[320,2048]{1,0:T(8,128)(2,1)S(1)}, u32[]{:S(2)}, u32[]{:S(2)}) %collective-permute-start.5) | collective-permute-done | bytes 1310752 | tf_op jit(solution)/shard_map/ppermute | solution.py:413
  83.1 0.0 collective-permute-done.3.refs_1_.refs_0_
  83.1 1.3 collective-permute-start.6
  84.4 0.0 slice-start
  84.4 0.2 take_rows.2
  84.6 0.0 slice-start.1
  84.6 0.8 collective-permute-start.8
  85.5 7.5 %hidden_grad_late_partial.1.refs_4_ = f32[320,3584]{1,0:T(8,128)} custom-call(bf16[320,2048]{1,0:T(8,128)(2,1)S(1)} %collective-permute-done.4.refs_0_.refs_1_, bf16[320,2048]{1,0:T(8,128)(2,1)S(1)} %collective-permute-done.5.refs_1_.refs_2_, bf16[3584,2048]{1,0:T(8,128)(2,1)S(1)} %get-tuple-element.51.refs_2_), custom_call_target="tpu_custom_call" | custom-call | flops 1 | bytes 1 | tf_op jit(solution)/shard_map/hidden_grad_late_partial/pallas_call | solution.py:307
  93.0 0.4 in_token_order.8.block
  93.4 0.0 slice-done
  93.4 0.0 slice-done.1
  93.4 14.5 %weight_grad.2.refs_0_ = bf16[3584,2048]{1,0:T(8,128)(2,1)S(1)} custom-call(bf16[640,3584]{1,0:T(8,128)(2,1)S(1)} %bitcast.9, bf16[640,2048]{1,0:T(8,128)(2,1)S(1)} %in_token_order.8.block), custom_call_target="tpu_custom_call" | custom-call | flops 1 | bytes 1 | tf_op jit(solution)/shard_map/weight_grad/pallas_call | solution.py:356
  107.9 0.6 mark.5.refs_3_
  108.5 0.0 collective-permute-done.8.refs_0_
  108.5 1.3 collective-permute-start.10
  109.8 4.0 %collective-permute-done.6.refs_2_.refs_1_ = bf16[320,2048]{1,0:T(8,128)(2,1)S(1)} collective-permute-done((bf16[320,2048]{1,0:T(8,128)(2,1)S(1)}, bf16[320,2048]{1,0:T(8,128)(2,1)S(1)}, u32[]{:S(2)}, u32[]{:S(2)}) %collective-permute-start.6) | collective-permute-done | bytes 1310752 | tf_op jit(solution)/shard_map/ppermute | solution.py:413
  113.8 4.4 %collective-permute-done.7.hidden = bf16[640,3584]{1,0:T(8,128)(2,1)S(1)} collective-permute-done((bf16[640,3584]{1,0:T(8,128)(2,1)}, bf16[640,3584]{1,0:T(8,128)(2,1)S(1)}, u32[]{:S(2)}, u32[]{:S(2)}) %collective-permute-start.7) | collective-permute-done | bytes 4587552 | tf_op jit(solution)/shard_map/ppermute | solution.py:398
  118.1 0.0 copy-start
  118.1 2.1 %copy-done = bf16[640,3584]{1,0:T(8,128)(2,1)} copy-done((bf16[640,3584]{1,0:T(8,128)(2,1)}, bf16[640,3584]{1,0:T(8,128)(2,1)S(1)}, u32[]{:S(2)}) %copy-start) | copy-done | bytes 4587544
  120.3 0.2 take_rows.3
  120.5 0.0 copy-start.1
  120.5 1.8 %collective-permute-start.11 = (bf16[160,2048]{1,0:T(8,128)(2,1)S(1)}, bf16[160,2048]{1,0:T(8,128)(2,1)S(1)}, u32[]{:S(2)}, u32[]{:S(2)}) collective-permute-start(bf16[160,2048]{1,0:T(8,128)(2,1)S(1)} %take_rows.3), channel_id=1, source_target_pairs={{0,2},{1,3},{2,0},{3,1},{4,6},{5,7},{6,4},{7,5},{8,10},{9,11},{10,... | collective-permute-start | bytes 1966088 | tf_op jit(solution)/shard_map/ppermute | solution.py:398
  122.3 0.3 in_token_order.9.block
  122.7 0.1 copy-done.1
  122.8 15.0 %weight_grad.3 = (bf16[3584,1024]{1,0:T(8,128)(2,1)}, bf16[3584,1024]{1,0:T(8,128)(2,1)S(1)}) custom-call(bf16[640,3584]{1,0:T(8,128)(2,1)S(1)} %copy-done.1, bf16[640,2048]{1,0:T(8,128)(2,1)S(1)} %in_token_order.9.block, bf16[3584,2048]{1,0:T(8,128)(2,1)S(1)} %weight_grad.2.refs_0_), custom_call_target="tpu_custom_call" | custom-call | flops 1 | bytes 1 | tf_op jit(solution)/shard_map/weight_grad/pallas_call | solution.py:356
  137.8 0.0 collective-permute-start.9
  137.8 0.0 collective-permute-done.10.refs_1_
  137.8 0.0 collective-permute-done.11.refs_2_
  137.8 11.8 %hidden_grad_late.1 = (bf16[640,3584]{1,0:T(8,128)(2,1)}, bf16[640,3584]{1,0:T(8,128)(2,1)}) custom-call(bf16[160,2048]{1,0:T(8,128)(2,1)S(1)} %collective-permute-done.8.refs_0_, bf16[160,2048]{1,0:T(8,128)(2,1)S(1)} %collective-permute-done.10.refs_1_, ...), custom_call_target="tpu_custom_call", output_to_operand_aliasing={{0}: (8, {}), {1}: (9, {})} | custom-call | flops 999999995904 | bytes 1000000000 | tf_op jit(solution)/shard_map/hidden_grad_late/pallas_call | solution.py:307
  149.5 0.2 collective-permute-done.9.b_ref
  149.8 7.2 %scaled_sum.1 = bf16[3584,1024]{1,0:T(8,128)(2,1)} custom-call(bf16[3584,1024]{1,0:T(8,128)(2,1)S(1)} %get-tuple-element.79.a_ref, bf16[3584,1024]{1,0:T(8,128)(2,1)} %collective-permute-done.9.b_ref), custom_call_target="tpu_custom_call" | custom-call | flops 1 | bytes 1 | tf_op jit(solution)/shard_map/scaled_sum/pallas_call | solution.py:375
  (1 shorter events, 0.0 us)
Async XLA Ops:
  2.1 18.6 %collective-permute-start = (bf16[160,2048]{1,0:T(8,128)(2,1)S(1)}, bf16[160,2048]{1,0:T(8,128)(2,1)S(1)}, u32[]{:S(2)}, u32[]{:S(2)}) collective-permute-start(bf16[160,2048]{1,0:T(8,128)(2,1)S(1)} %get-tuple-element.42.refs_1_.refs_0_), channel_id=1, source_target_pairs={{0,2},{1,3},{2,0},{3,1},{4,6},{5,7},{6,4},{7,5},{8,10},{9,11},{10,... | collective-permute-start | bytes 1966088 | tf_op jit(solution)/shard_map/ppermute | solution.py:398
  5.1 18.8 %collective-permute-start.2 = (bf16[160,2048]{1,0:T(8,128)(2,1)S(1)}, bf16[160,2048]{1,0:T(8,128)(2,1)S(1)}, u32[]{:S(2)}, u32[]{:S(2)}) collective-permute-start(bf16[160,2048]{1,0:T(8,128)(2,1)S(1)} %get-tuple-element.43.refs_0_), channel_id=1, source_target_pairs={{0,4},{4,0},{8,12},{12,8},{1,5},{5,1},{9,13},{13,9},{2,6},{6,2},{1... | collective-permute-start | bytes 1966088 | tf_op jit(solution)/shard_map/ppermute | solution.py:411
  16.2 102.0 %collective-permute-start.7 = (bf16[640,3584]{1,0:T(8,128)(2,1)}, bf16[640,3584]{1,0:T(8,128)(2,1)S(1)}, u32[]{:S(2)}, u32[]{:S(2)}) collective-permute-start(bf16[640,3584]{1,0:T(8,128)(2,1)} %hidden.1), channel_id=1, source_target_pairs={{0,2},{1,3},{2,0},{3,1},{4,6},{5,7},{6,4},{7,5},{8,10},{9,11},{10,... | collective-permute-start | bytes 13762568 | tf_op jit(solution)/shard_map/ppermute | solution.py:398
  21.1 29.2 %collective-permute-start.1 = (bf16[320,2048]{1,0:T(8,128)(2,1)S(1)}, bf16[320,2048]{1,0:T(8,128)(2,1)S(1)}, u32[]{:S(2)}, u32[]{:S(2)}) collective-permute-start(bf16[320,2048]{1,0:T(8,128)(2,1)S(1)} %stack.1), channel_id=1, source_target_pairs={{0,4},{4,0},{8,12},{12,8},{1,5},{5,1},{9,13},{13,9},{2,6},{6,2},{1... | collective-permute-start | bytes 3932168 | tf_op jit(solution)/shard_map/ppermute | solution.py:411
  24.4 27.0 %collective-permute-start.4 = (bf16[320,2048]{1,0:T(8,128)(2,1)S(1)}, bf16[320,2048]{1,0:T(8,128)(2,1)S(1)}, u32[]{:S(2)}, u32[]{:S(2)}) collective-permute-start(bf16[320,2048]{1,0:T(8,128)(2,1)S(1)} %in_token_order.6.refs_0_), channel_id=1, source_target_pairs={{4,8},{8,4},{5,9},{9,5},{6,10},{10,6},{7,11},{11,7},{20,24},{24,20... | collective-permute-start | bytes 3932168 | tf_op jit(solution)/shard_map/ppermute | solution.py:412
  51.4 31.6 %collective-permute-start.5 = (bf16[320,2048]{1,0:T(8,128)(2,1)S(1)}, bf16[320,2048]{1,0:T(8,128)(2,1)S(1)}, u32[]{:S(2)}, u32[]{:S(2)}) collective-permute-start(bf16[320,2048]{1,0:T(8,128)(2,1)S(1)} %collective-permute-done.4.refs_0_.refs_1_), channel_id=1, source_target_pairs={{4,0},{8,12},{5,1},{9,13},{6,2},{10,14},{7,3},{11,15},{20,16},{24,... | collective-permute-start | bytes 3932168 | tf_op jit(solution)/shard_map/ppermute | solution.py:413
  53.3 29.8 %collective-permute-start.3 = (bf16[320,2048]{1,0:T(8,128)(2,1)S(1)}, bf16[320,2048]{1,0:T(8,128)(2,1)S(1)}, u32[]{:S(2)}, u32[]{:S(2)}) collective-permute-start(bf16[320,2048]{1,0:T(8,128)(2,1)S(1)} %in_token_order.5.refs_0_), channel_id=1, source_target_pairs={{4,8},{8,4},{5,9},{9,5},{6,10},{10,6},{7,11},{11,7},{20,24},{24,20... | collective-permute-start | bytes 3932168 | tf_op jit(solution)/shard_map/ppermute | solution.py:412
  83.1 30.7 %collective-permute-start.6 = (bf16[320,2048]{1,0:T(8,128)(2,1)S(1)}, bf16[320,2048]{1,0:T(8,128)(2,1)S(1)}, u32[]{:S(2)}, u32[]{:S(2)}) collective-permute-start(bf16[320,2048]{1,0:T(8,128)(2,1)S(1)} %collective-permute-done.3.refs_1_.refs_0_), channel_id=1, source_target_pairs={{4,0},{8,12},{5,1},{9,13},{6,2},{10,14},{7,3},{11,15},{20,16},{24,... | collective-permute-start | bytes 3932168 | tf_op jit(solution)/shard_map/ppermute | solution.py:413
  84.4 9.0 %slice-start = ((s8[4587520]{0:T(1024)(128)(4,1)}), s8[4194304]{0:T(1024)(128)(4,1)S(1)}, s32[]{:S(2)}) async-start(s8[4587520]{0:T(1024)(128)(4,1)} %bitcast.8), calls=%async_computation | async-start | bytes 8388608
  84.6 8.8 %slice-start.1 = ((s8[4587520]{0:T(1024)(128)(4,1)}), s8[393216]{0:T(1024)(128)(4,1)S(1)}, s32[]{:S(2)}) async-start(s8[4587520]{0:T(1024)(128)(4,1)} %bitcast.8), calls=%async_computation.1 | async-start | bytes 786432
  84.6 23.9 %collective-permute-start.8 = (bf16[160,2048]{1,0:T(8,128)(2,1)S(1)}, bf16[160,2048]{1,0:T(8,128)(2,1)S(1)}, u32[]{:S(2)}, u32[]{:S(2)}) collective-permute-start(bf16[160,2048]{1,0:T(8,128)(2,1)S(1)} %take_rows.2), channel_id=1, source_target_pairs={{4,8},{8,4},{5,9},{9,5},{6,10},{10,6},{7,11},{11,7},{20,24},{24,20... | collective-permute-start | bytes 1966088 | tf_op jit(solution)/shard_map/ppermute | solution.py:412
  108.5 29.3 %collective-permute-start.10 = (bf16[160,2048]{1,0:T(8,128)(2,1)S(1)}, bf16[160,2048]{1,0:T(8,128)(2,1)S(1)}, u32[]{:S(2)}, u32[]{:S(2)}) collective-permute-start(bf16[160,2048]{1,0:T(8,128)(2,1)S(1)} %collective-permute-done.8.refs_0_), channel_id=1, source_target_pairs={{4,0},{8,12},{5,1},{9,13},{6,2},{10,14},{7,3},{11,15},{20,16},{24,... | collective-permute-start | bytes 1966088 | tf_op jit(solution)/shard_map/ppermute | solution.py:413
  118.1 2.1 %copy-start = (bf16[640,3584]{1,0:T(8,128)(2,1)}, bf16[640,3584]{1,0:T(8,128)(2,1)S(1)}, u32[]{:S(2)}) copy-start(bf16[640,3584]{1,0:T(8,128)(2,1)S(1)} %collective-permute-done.7.hidden) | copy-start | bytes 13762564
  120.5 2.3 %copy-start.1 = (bf16[640,3584]{1,0:T(8,128)(2,1)S(1)}, bf16[640,3584]{1,0:T(8,128)(2,1)}, u32[]{:S(2)}) copy-start(bf16[640,3584]{1,0:T(8,128)(2,1)} %copy-done) | copy-start | bytes 13762564
  120.5 17.3 %collective-permute-start.11 = (bf16[160,2048]{1,0:T(8,128)(2,1)S(1)}, bf16[160,2048]{1,0:T(8,128)(2,1)S(1)}, u32[]{:S(2)}, u32[]{:S(2)}) collective-permute-start(bf16[160,2048]{1,0:T(8,128)(2,1)S(1)} %take_rows.3), channel_id=1, source_target_pairs={{0,2},{1,3},{2,0},{3,1},{4,6},{5,7},{6,4},{7,5},{8,10},{9,11},{10,... | collective-permute-start | bytes 1966088 | tf_op jit(solution)/shard_map/ppermute | solution.py:398
  137.8 12.0 %collective-permute-start.9 = (bf16[3584,1024]{1,0:T(8,128)(2,1)}, bf16[3584,1024]{1,0:T(8,128)(2,1)}, u32[]{:S(2)}, u32[]{:S(2)}) collective-permute-start(bf16[3584,1024]{1,0:T(8,128)(2,1)} %get-tuple-element.72.refs_7_), channel_id=1, source_target_pairs={{0,1},{1,0},{2,3},{3,2},{4,5},{5,4},{6,7},{7,6},{8,9},{9,8},{10,11... | collective-permute-start | bytes 22020104 | tf_op jit(solution)/shard_map/ppermute | solution.py:403

commit v4 on v3

--- a/solution.py
+++ b/solution.py
@@ -269,7 +269,7 @@
 def hidden_grad(half, streams, weights, tok, partial=None, by=None, outs=None, wait_for=()):
     ff = weights[0].shape[0]
     rows = tok if half == "all" else tok // 2
-    tile = pick_tile(ff, 896 if by is None else 512)
+    tile = pick_tile(ff, 512 if half == "early" else 896)
 
     def place(i):
         pair = lax.axis_index("tensor") // 2
@@ -320,7 +320,7 @@
         out_shape=out_shape,
         input_output_aliases=aliases,
         cost_estimate=LONG if outs is not None else SHORT,
-        compiler_params=pltpu.CompilerParams(vmem_limit_bytes=VMEM_LIMIT),
+        compiler_params=pltpu.CompilerParams(vmem_limit_bytes=VMEM_LIMIT * (3 if outs is not None else 2) // 2),
         name="hidden_grad_" + half + ("" if by is not None else "_partial"),
     )(*args)
 

time: 158 us -> 158 us (level)
  no operation moved by 1% of the time
where the time goes in v4:
time: 158 us; the launch traced here: 157 us
  Pallas kernels  94.4 us (60%)
  waiting for transfers between devices  42.7 us (27%)
  starting transfers between devices  15.3 us (10%)
  local copies, waits for them, and re-layouts  3.72 us (2%)
    pallas_call x3, Pallas kernels, hidden_grad(): pl.pallas_call(functools.partial(hidden_grad_kernel, half, tuple((len(s)...  33.2 us
    pallas_call x2, Pallas kernels, weight_grad(): pl.pallas_call(functools.partial(weight_grad_kernel, tile, start is not N...  29.5 us
    ppermute x3, waiting for transfers between devices, on_device(): to_ends = lambda v: lax.ppermute(v, 'tensor', [(1, 0), (2, 3)])  18.5 us
    ppermute x2, waiting for transfers between devices, on_device(): swap_pair = lambda v: lax.ppermute(v, 'tensor', both_ways((0, 1), (2, 3)))  15.1 us
    pallas_call x1, Pallas kernels, load_weight(): pl.pallas_call(load_weight_kernel, in_specs=[ANY_SPEC], out_specs=[VMEM_S...  9.98 us
    pallas_call x1, Pallas kernels, hidden_of(): pl.pallas_call(hidden_kernel, grid=(tok // rows,), in_specs=[spec] * 2, o...  9.49 us
    ppermute x3, waiting for transfers between devices, shift(): lax.ppermute(value, 'dp', [(2 * c + k, 2 * ((c + s) % chips) + k) for c i...  8.32 us
    pallas_call x1, Pallas kernels, scaled_sum(): pl.pallas_call(functools.partial(add_kernel, scale), grid=(rows // spec.b...  7.24 us
  transfers between devices with their start and end apart: 12, of which 6 were waited for; matrix products, arithmetic and copies ran while one was open for 0% of the time, Pallas kernels for 56%

profile of v4, /device:TPU:0, one launch (start us, length us, event | category | flops | bytes accessed | tf_op | source)
XLA Modules:
  0.0 157.0 jit_solution(14151174257501873890)
XLA Ops:
  0.7 1.4 dynamic-slice_bitcast_fusion
  2.1 3.0 %collective-permute-start = (bf16[160,2048]{1,0:T(8,128)(2,1)S(1)}, bf16[160,2048]{1,0:T(8,128)(2,1)S(1)}, u32[]{:S(2)}, u32[]{:S(2)}) collective-permute-start(bf16[160,2048]{1,0:T(8,128)(2,1)S(1)} %get-tuple-element.42.refs_1_.refs_0_), channel_id=1, source_target_pairs={{0,2},{1,3},{2,0},{3,1},{4,6},{5,7},{6,4},{7,5},{8,10},{9,11},{10,... | collective-permute-start | bytes 1966088 | tf_op jit(solution)/shard_map/ppermute | solution.py:398
  5.1 1.6 %collective-permute-start.2 = (bf16[160,2048]{1,0:T(8,128)(2,1)S(1)}, bf16[160,2048]{1,0:T(8,128)(2,1)S(1)}, u32[]{:S(2)}, u32[]{:S(2)}) collective-permute-start(bf16[160,2048]{1,0:T(8,128)(2,1)S(1)} %get-tuple-element.43.refs_0_), channel_id=1, source_target_pairs={{0,4},{4,0},{8,12},{12,8},{1,5},{5,1},{9,13},{13,9},{2,6},{6,2},{1... | collective-permute-start | bytes 1966088 | tf_op jit(solution)/shard_map/ppermute | solution.py:411
  6.7 9.5 %hidden.1 = bf16[640,3584]{1,0:T(8,128)(2,1)} custom-call(bf16[640,3584]{1,0:T(8,128)(2,1)} %bitcast.10, bf16[640,3584]{1,0:T(8,128)(2,1)} %bitcast.13), custom_call_target="tpu_custom_call" | custom-call | flops 1 | bytes 1 | tf_op jit(solution)/shard_map/hidden/pallas_call | solution.py:223
  16.2 0.5 collective-permute-start.7
  16.7 4.0 %collective-permute-done.refs_0_ = bf16[160,2048]{1,0:T(8,128)(2,1)S(1)} collective-permute-done((bf16[160,2048]{1,0:T(8,128)(2,1)S(1)}, bf16[160,2048]{1,0:T(8,128)(2,1)S(1)}, u32[]{:S(2)}, u32[]{:S(2)}) %collective-permute-start) | collective-permute-done | bytes 655392 | tf_op jit(solution)/shard_map/ppermute | solution.py:398
  20.6 0.4 stack.1
  21.1 2.2 %collective-permute-start.1 = (bf16[320,2048]{1,0:T(8,128)(2,1)S(1)}, bf16[320,2048]{1,0:T(8,128)(2,1)S(1)}, u32[]{:S(2)}, u32[]{:S(2)}) collective-permute-start(bf16[320,2048]{1,0:T(8,128)(2,1)S(1)} %stack.1), channel_id=1, source_target_pairs={{0,4},{4,0},{8,12},{12,8},{1,5},{5,1},{9,13},{13,9},{2,6},{6,2},{1... | collective-permute-start | bytes 3932168 | tf_op jit(solution)/shard_map/ppermute | solution.py:411
  23.3 0.6 mark.3.refs_2_
  23.9 0.0 collective-permute-done.2.refs_1_
  23.9 0.6 in_token_order.6.refs_0_
  24.4 0.7 collective-permute-start.4
  25.2 10.0 %load_weight.1 = (bf16[3584,2048]{1,0:T(8,128)(2,1)S(1)}, bf16[3584,2048]{1,0:T(8,128)(2,1)S(1)}, f32[8,128]{1,0:T(8,128)}) custom-call(bf16[3584,4096]{1,0:T(8,128)(2,1)} %weight), custom_call_target="tpu_custom_call" | custom-call | flops 1 | bytes 1 | tf_op jit(solution)/shard_map/load_weight/pallas_call | solution.py:202
  35.2 15.1 %collective-permute-done.1.refs_1_ = bf16[320,2048]{1,0:T(8,128)(2,1)S(1)} collective-permute-done((bf16[320,2048]{1,0:T(8,128)(2,1)S(1)}, bf16[320,2048]{1,0:T(8,128)(2,1)S(1)}, u32[]{:S(2)}, u32[]{:S(2)}) %collective-permute-start.1) | collective-permute-done | bytes 1310752 | tf_op jit(solution)/shard_map/ppermute | solution.py:411
  50.3 0.6 in_token_order.7.refs_0_.refs_1_
  50.8 0.6 mark.4.refs_6_
  51.4 0.0 collective-permute-done.4.refs_0_.refs_1_
  51.4 1.3 collective-permute-start.5
  52.7 0.6 in_token_order.5.refs_0_
  53.3 0.7 collective-permute-start.3
  54.1 14.5 %hidden_grad_early.1 = (bf16[640,3584]{1,0:T(8,128)(2,1)}, bf16[640,3584]{1,0:T(8,128)(2,1)}) custom-call(bf16[320,2048]{1,0:T(8,128)(2,1)S(1)} %in_token_order.6.refs_0_, bf16[320,2048]{1,0:T(8,128)(2,1)S(1)} %in_token_order.7.refs_0_.refs_1_, bf16[3584,2048]{1,0:T(8,128)(2,1)S(1)} %get-tuple-element.51.refs_2_, ...), custom_call_target="tpu_custom_call" | custom-call | flops 1 | bytes 1 | tf_op jit(solution)/shard_map/hidden_grad_early/pallas_call | solution.py:307
  68.6 14.5 %collective-permute-done.5.refs_1_.refs_2_ = bf16[320,2048]{1,0:T(8,128)(2,1)S(1)} collective-permute-done((bf16[320,2048]{1,0:T(8,128)(2,1)S(1)}, bf16[320,2048]{1,0:T(8,128)(2,1)S(1)}, u32[]{:S(2)}, u32[]{:S(2)}) %collective-permute-start.5) | collective-permute-done | bytes 1310752 | tf_op jit(solution)/shard_map/ppermute | solution.py:413
  83.1 0.0 collective-permute-done.3.refs_1_.refs_0_
  83.1 1.3 collective-permute-start.6
  84.4 0.0 slice-start
  84.4 0.2 take_rows.2
  84.6 0.0 slice-start.1
  84.6 0.8 collective-permute-start.8
  85.5 7.5 %hidden_grad_late_partial.1.refs_4_ = f32[320,3584]{1,0:T(8,128)} custom-call(bf16[320,2048]{1,0:T(8,128)(2,1)S(1)} %collective-permute-done.4.refs_0_.refs_1_, bf16[320,2048]{1,0:T(8,128)(2,1)S(1)} %collective-permute-done.5.refs_1_.refs_2_, bf16[3584,2048]{1,0:T(8,128)(2,1)S(1)} %get-tuple-element.51.refs_2_), custom_call_target="tpu_custom_call" | custom-call | flops 1 | bytes 1 | tf_op jit(solution)/shard_map/hidden_grad_late_partial/pallas_call | solution.py:307
  93.0 0.4 in_token_order.8.block
  93.4 0.0 slice-done
  93.4 0.0 slice-done.1
  93.4 14.5 %weight_grad.2.refs_0_ = bf16[3584,2048]{1,0:T(8,128)(2,1)S(1)} custom-call(bf16[640,3584]{1,0:T(8,128)(2,1)S(1)} %bitcast.9, bf16[640,2048]{1,0:T(8,128)(2,1)S(1)} %in_token_order.8.block), custom_call_target="tpu_custom_call" | custom-call | flops 1 | bytes 1 | tf_op jit(solution)/shard_map/weight_grad/pallas_call | solution.py:356
  107.9 0.6 mark.5.refs_3_
  108.5 0.0 collective-permute-done.8.refs_0_
  108.5 1.3 collective-permute-start.10
  109.8 4.0 %collective-permute-done.6.refs_2_.refs_1_ = bf16[320,2048]{1,0:T(8,128)(2,1)S(1)} collective-permute-done((bf16[320,2048]{1,0:T(8,128)(2,1)S(1)}, bf16[320,2048]{1,0:T(8,128)(2,1)S(1)}, u32[]{:S(2)}, u32[]{:S(2)}) %collective-permute-start.6) | collective-permute-done | bytes 1310752 | tf_op jit(solution)/shard_map/ppermute | solution.py:413
  113.8 4.4 %collective-permute-done.7.hidden = bf16[640,3584]{1,0:T(8,128)(2,1)S(1)} collective-permute-done((bf16[640,3584]{1,0:T(8,128)(2,1)}, bf16[640,3584]{1,0:T(8,128)(2,1)S(1)}, u32[]{:S(2)}, u32[]{:S(2)}) %collective-permute-start.7) | collective-permute-done | bytes 4587552 | tf_op jit(solution)/shard_map/ppermute | solution.py:398
  118.1 0.0 copy-start
  118.1 2.1 %copy-done = bf16[640,3584]{1,0:T(8,128)(2,1)} copy-done((bf16[640,3584]{1,0:T(8,128)(2,1)}, bf16[640,3584]{1,0:T(8,128)(2,1)S(1)}, u32[]{:S(2)}) %copy-start) | copy-done | bytes 4587544
  120.3 0.2 take_rows.3
  120.5 0.0 copy-start.1
  120.5 1.8 %collective-permute-start.11 = (bf16[160,2048]{1,0:T(8,128)(2,1)S(1)}, bf16[160,2048]{1,0:T(8,128)(2,1)S(1)}, u32[]{:S(2)}, u32[]{:S(2)}) collective-permute-start(bf16[160,2048]{1,0:T(8,128)(2,1)S(1)} %take_rows.3), channel_id=1, source_target_pairs={{0,2},{1,3},{2,0},{3,1},{4,6},{5,7},{6,4},{7,5},{8,10},{9,11},{10,... | collective-permute-start | bytes 1966088 | tf_op jit(solution)/shard_map/ppermute | solution.py:398
  122.3 0.3 in_token_order.9.block
  122.7 0.1 copy-done.1
  122.8 15.0 %weight_grad.3 = (bf16[3584,1024]{1,0:T(8,128)(2,1)}, bf16[3584,1024]{1,0:T(8,128)(2,1)S(1)}) custom-call(bf16[640,3584]{1,0:T(8,128)(2,1)S(1)} %copy-done.1, bf16[640,2048]{1,0:T(8,128)(2,1)S(1)} %in_token_order.9.block, bf16[3584,2048]{1,0:T(8,128)(2,1)S(1)} %weight_grad.2.refs_0_), custom_call_target="tpu_custom_call" | custom-call | flops 1 | bytes 1 | tf_op jit(solution)/shard_map/weight_grad/pallas_call | solution.py:356
  137.8 0.0 collective-permute-start.9
  137.8 0.0 collective-permute-done.10.refs_1_
  137.8 0.0 collective-permute-done.11.refs_2_
  137.8 11.2 %hidden_grad_late.1 = (bf16[640,3584]{1,0:T(8,128)(2,1)}, bf16[640,3584]{1,0:T(8,128)(2,1)}) custom-call(bf16[160,2048]{1,0:T(8,128)(2,1)S(1)} %collective-permute-done.8.refs_0_, bf16[160,2048]{1,0:T(8,128)(2,1)S(1)} %collective-permute-done.10.refs_1_, ...), custom_call_target="tpu_custom_call", output_to_operand_aliasing={{0}: (8, {}), {1}: (9, {})} | custom-call | flops 999999995904 | bytes 1000000000 | tf_op jit(solution)/shard_map/hidden_grad_late/pallas_call | solution.py:307
  149.0 0.8 collective-permute-done.9.b_ref
  149.8 7.2 %scaled_sum.1 = bf16[3584,1024]{1,0:T(8,128)(2,1)} custom-call(bf16[3584,1024]{1,0:T(8,128)(2,1)S(1)} %get-tuple-element.79.a_ref, bf16[3584,1024]{1,0:T(8,128)(2,1)} %collective-permute-done.9.b_ref), custom_call_target="tpu_custom_call" | custom-call | flops 1 | bytes 1 | tf_op jit(solution)/shard_map/scaled_sum/pallas_call | solution.py:375
  (1 shorter events, 0.0 us)
Async XLA Ops:
  2.1 18.6 %collective-permute-start = (bf16[160,2048]{1,0:T(8,128)(2,1)S(1)}, bf16[160,2048]{1,0:T(8,128)(2,1)S(1)}, u32[]{:S(2)}, u32[]{:S(2)}) collective-permute-start(bf16[160,2048]{1,0:T(8,128)(2,1)S(1)} %get-tuple-element.42.refs_1_.refs_0_), channel_id=1, source_target_pairs={{0,2},{1,3},{2,0},{3,1},{4,6},{5,7},{6,4},{7,5},{8,10},{9,11},{10,... | collective-permute-start | bytes 1966088 | tf_op jit(solution)/shard_map/ppermute | solution.py:398
  5.1 18.8 %collective-permute-start.2 = (bf16[160,2048]{1,0:T(8,128)(2,1)S(1)}, bf16[160,2048]{1,0:T(8,128)(2,1)S(1)}, u32[]{:S(2)}, u32[]{:S(2)}) collective-permute-start(bf16[160,2048]{1,0:T(8,128)(2,1)S(1)} %get-tuple-element.43.refs_0_), channel_id=1, source_target_pairs={{0,4},{4,0},{8,12},{12,8},{1,5},{5,1},{9,13},{13,9},{2,6},{6,2},{1... | collective-permute-start | bytes 1966088 | tf_op jit(solution)/shard_map/ppermute | solution.py:411
  16.2 102.0 %collective-permute-start.7 = (bf16[640,3584]{1,0:T(8,128)(2,1)}, bf16[640,3584]{1,0:T(8,128)(2,1)S(1)}, u32[]{:S(2)}, u32[]{:S(2)}) collective-permute-start(bf16[640,3584]{1,0:T(8,128)(2,1)} %hidden.1), channel_id=1, source_target_pairs={{0,2},{1,3},{2,0},{3,1},{4,6},{5,7},{6,4},{7,5},{8,10},{9,11},{10,... | collective-permute-start | bytes 13762568 | tf_op jit(solution)/shard_map/ppermute | solution.py:398
  21.1 29.2 %collective-permute-start.1 = (bf16[320,2048]{1,0:T(8,128)(2,1)S(1)}, bf16[320,2048]{1,0:T(8,128)(2,1)S(1)}, u32[]{:S(2)}, u32[]{:S(2)}) collective-permute-start(bf16[320,2048]{1,0:T(8,128)(2,1)S(1)} %stack.1), channel_id=1, source_target_pairs={{0,4},{4,0},{8,12},{12,8},{1,5},{5,1},{9,13},{13,9},{2,6},{6,2},{1... | collective-permute-start | bytes 3932168 | tf_op jit(solution)/shard_map/ppermute | solution.py:411
  24.4 27.0 %collective-permute-start.4 = (bf16[320,2048]{1,0:T(8,128)(2,1)S(1)}, bf16[320,2048]{1,0:T(8,128)(2,1)S(1)}, u32[]{:S(2)}, u32[]{:S(2)}) collective-permute-start(bf16[320,2048]{1,0:T(8,128)(2,1)S(1)} %in_token_order.6.refs_0_), channel_id=1, source_target_pairs={{4,8},{8,4},{5,9},{9,5},{6,10},{10,6},{7,11},{11,7},{20,24},{24,20... | collective-permute-start | bytes 3932168 | tf_op jit(solution)/shard_map/ppermute | solution.py:412
  51.4 31.6 %collective-permute-start.5 = (bf16[320,2048]{1,0:T(8,128)(2,1)S(1)}, bf16[320,2048]{1,0:T(8,128)(2,1)S(1)}, u32[]{:S(2)}, u32[]{:S(2)}) collective-permute-start(bf16[320,2048]{1,0:T(8,128)(2,1)S(1)} %collective-permute-done.4.refs_0_.refs_1_), channel_id=1, source_target_pairs={{4,0},{8,12},{5,1},{9,13},{6,2},{10,14},{7,3},{11,15},{20,16},{24,... | collective-permute-start | bytes 3932168 | tf_op jit(solution)/shard_map/ppermute | solution.py:413
  53.3 29.8 %collective-permute-start.3 = (bf16[320,2048]{1,0:T(8,128)(2,1)S(1)}, bf16[320,2048]{1,0:T(8,128)(2,1)S(1)}, u32[]{:S(2)}, u32[]{:S(2)}) collective-permute-start(bf16[320,2048]{1,0:T(8,128)(2,1)S(1)} %in_token_order.5.refs_0_), channel_id=1, source_target_pairs={{4,8},{8,4},{5,9},{9,5},{6,10},{10,6},{7,11},{11,7},{20,24},{24,20... | collective-permute-start | bytes 3932168 | tf_op jit(solution)/shard_map/ppermute | solution.py:412
  83.1 30.7 %collective-permute-start.6 = (bf16[320,2048]{1,0:T(8,128)(2,1)S(1)}, bf16[320,2048]{1,0:T(8,128)(2,1)S(1)}, u32[]{:S(2)}, u32[]{:S(2)}) collective-permute-start(bf16[320,2048]{1,0:T(8,128)(2,1)S(1)} %collective-permute-done.3.refs_1_.refs_0_), channel_id=1, source_target_pairs={{4,0},{8,12},{5,1},{9,13},{6,2},{10,14},{7,3},{11,15},{20,16},{24,... | collective-permute-start | bytes 3932168 | tf_op jit(solution)/shard_map/ppermute | solution.py:413
  84.4 9.0 %slice-start = ((s8[4587520]{0:T(1024)(128)(4,1)}), s8[4194304]{0:T(1024)(128)(4,1)S(1)}, s32[]{:S(2)}) async-start(s8[4587520]{0:T(1024)(128)(4,1)} %bitcast.8), calls=%async_computation | async-start | bytes 8388608
  84.6 8.8 %slice-start.1 = ((s8[4587520]{0:T(1024)(128)(4,1)}), s8[393216]{0:T(1024)(128)(4,1)S(1)}, s32[]{:S(2)}) async-start(s8[4587520]{0:T(1024)(128)(4,1)} %bitcast.8), calls=%async_computation.1 | async-start | bytes 786432
  84.6 23.9 %collective-permute-start.8 = (bf16[160,2048]{1,0:T(8,128)(2,1)S(1)}, bf16[160,2048]{1,0:T(8,128)(2,1)S(1)}, u32[]{:S(2)}, u32[]{:S(2)}) collective-permute-start(bf16[160,2048]{1,0:T(8,128)(2,1)S(1)} %take_rows.2), channel_id=1, source_target_pairs={{4,8},{8,4},{5,9},{9,5},{6,10},{10,6},{7,11},{11,7},{20,24},{24,20... | collective-permute-start | bytes 1966088 | tf_op jit(solution)/shard_map/ppermute | solution.py:412
  108.5 29.3 %collective-permute-start.10 = (bf16[160,2048]{1,0:T(8,128)(2,1)S(1)}, bf16[160,2048]{1,0:T(8,128)(2,1)S(1)}, u32[]{:S(2)}, u32[]{:S(2)}) collective-permute-start(bf16[160,2048]{1,0:T(8,128)(2,1)S(1)} %collective-permute-done.8.refs_0_), channel_id=1, source_target_pairs={{4,0},{8,12},{5,1},{9,13},{6,2},{10,14},{7,3},{11,15},{20,16},{24,... | collective-permute-start | bytes 1966088 | tf_op jit(solution)/shard_map/ppermute | solution.py:413
  118.1 2.1 %copy-start = (bf16[640,3584]{1,0:T(8,128)(2,1)}, bf16[640,3584]{1,0:T(8,128)(2,1)S(1)}, u32[]{:S(2)}) copy-start(bf16[640,3584]{1,0:T(8,128)(2,1)S(1)} %collective-permute-done.7.hidden) | copy-start | bytes 13762564
  120.5 2.3 %copy-start.1 = (bf16[640,3584]{1,0:T(8,128)(2,1)S(1)}, bf16[640,3584]{1,0:T(8,128)(2,1)}, u32[]{:S(2)}) copy-start(bf16[640,3584]{1,0:T(8,128)(2,1)} %copy-done) | copy-start | bytes 13762564
  120.5 17.3 %collective-permute-start.11 = (bf16[160,2048]{1,0:T(8,128)(2,1)S(1)}, bf16[160,2048]{1,0:T(8,128)(2,1)S(1)}, u32[]{:S(2)}, u32[]{:S(2)}) collective-permute-start(bf16[160,2048]{1,0:T(8,128)(2,1)S(1)} %take_rows.3), channel_id=1, source_target_pairs={{0,2},{1,3},{2,0},{3,1},{4,6},{5,7},{6,4},{7,5},{8,10},{9,11},{10,... | collective-permute-start | bytes 1966088 | tf_op jit(solution)/shard_map/ppermute | solution.py:398
  137.8 12.0 %collective-permute-start.9 = (bf16[3584,1024]{1,0:T(8,128)(2,1)}, bf16[3584,1024]{1,0:T(8,128)(2,1)}, u32[]{:S(2)}, u32[]{:S(2)}) collective-permute-start(bf16[3584,1024]{1,0:T(8,128)(2,1)} %get-tuple-element.72.refs_7_), channel_id=1, source_target_pairs={{0,1},{1,0},{2,3},{3,2},{4,5},{5,4},{6,7},{7,6},{8,9},{9,8},{10,11... | collective-permute-start | bytes 22020104 | tf_op jit(solution)/shard_map/ppermute | solution.py:403
